TPU v7x, 32 devices: a whole 2x2x4 slice. The times are simulated.
32 devices in a mesh: dp: 4 (over y, x), ctx: 8 (over z, core).
Axes of the slice: x: 2, y: 2, z: 4, core: 2. Of those that a mesh axis runs over, the one named last changes fastest.
Arguments:
- tokens: bfloat16 [8, 1024, 768], P('dp', 'ctx'), may hold values from -6 to 6
- segments: int32 [8, 1024], P('dp', 'ctx'), may hold values from 0 to 7, as said below
- cotangent: bfloat16 [8, 1024, 768], P('dp', 'ctx'), may hold values from -6 to 6
- ln1_gain: bfloat16 [768], P(('dp', 'ctx')), may hold values from 0.5 to 1.5
- ln1_bias: bfloat16 [768], P(('dp', 'ctx')), may hold values from -2 to 2
- w_qkv: bfloat16 [768, 2304], P(('dp', 'ctx')), may hold values from -0.21875 to 0.21875
- bias_query: bfloat16 [768], P(('dp', 'ctx')), may hold values from -3 to 3
- bias_value: bfloat16 [768], P(('dp', 'ctx')), may hold values from -3 to 3
- w_out: bfloat16 [768, 768], P(('dp', 'ctx')), may hold values from -1.75 to 1.75
- bias_out: bfloat16 [768], P(('dp', 'ctx')), may hold values from -3 to 3
- ln2_gain: bfloat16 [768], P(('dp', 'ctx')), may hold values from 0.5 to 1.5
- ln2_bias: bfloat16 [768], P(('dp', 'ctx')), may hold values from -2 to 2
- w_up: bfloat16 [768, 3072], P(('dp', 'ctx')), may hold values from -0.21875 to 0.21875
- bias_up: bfloat16 [3072], P(('dp', 'ctx')), may hold values from -3 to 3
- w_down: bfloat16 [3072, 768], P(('dp', 'ctx')), may hold values from -0.109375 to 0.109375
- bias_down: bfloat16 [768], P(('dp', 'ctx')), may hold values from -3 to 3
Outputs:
- output: bfloat16 [8, 1024, 768], P('dp', 'ctx')
- grad_tokens: bfloat16 [8, 1024, 768], P('dp', 'ctx')
- grad_ln1_gain: float32 [768], P(('dp', 'ctx'))
- grad_ln1_bias: float32 [768], P(('dp', 'ctx'))
- grad_w_qkv: float32 [768, 2304], P(('dp', 'ctx'))
- grad_bias_query: float32 [768], P(('dp', 'ctx'))
- grad_bias_value: float32 [768], P(('dp', 'ctx'))
- grad_w_out: float32 [768, 768], P(('dp', 'ctx'))
- grad_bias_out: float32 [768], P(('dp', 'ctx'))
- grad_ln2_gain: float32 [768], P(('dp', 'ctx'))
- grad_ln2_bias: float32 [768], P(('dp', 'ctx'))
- grad_w_up: float32 [768, 3072], P(('dp', 'ctx'))
- grad_bias_up: float32 [3072], P(('dp', 'ctx'))
- grad_w_down: float32 [3072, 768], P(('dp', 'ctx'))
- grad_bias_down: float32 [768], P(('dp', 'ctx'))
Inputs may be any that keep to these rules, and one draw needn't show every extreme that they name: `segments`: along each sequence the document number starts at 0 and rises by one where a new document begins; documents hold 128 to 512 tokens, the last of a sequence possibly fewer. Of the 2 sequences of each dp index, one is a single document; in one dp index a sequence consists of documents of exactly 128 tokens but its last.
All inputs are finite; a program needn't handle non-finite values.
Results may differ from a plain program's by a relative error of at most 0.035.
Values may be sent and summed in bfloat16 or wider, within the bound.
No kernel may reach another device: no remote copies, remote signals or barrier semaphores. Data moves between devices by JAX's collectives and lax.ppermute only.
A program may use at most 256 MiB of HBM per device.

v0:
```python
import jax
import jax.numpy as jnp
from jax import lax
from jax.sharding import PartitionSpec as P

HEADS = 12
HEAD_DIM = 64


EPSILON = 1e-05
NEGATIVE = -1e30
SCALING = 0.125


def layer_norm(values, gain_vec, shift_vec):
    center = values - jnp.mean(values, axis=-1, keepdims=True)
    spread = jnp.mean(center * center, axis=-1, keepdims=True)
    return center * lax.rsqrt(spread + EPSILON) * gain_vec + shift_vec


def split_heads(tensor):
    return tensor.reshape(tensor.shape[0], tensor.shape[1], HEADS, HEAD_DIM)


def visible(seg_query, seg_key, place_query, place_key):
    same_doc = seg_query[:, :, None] == seg_key[:, None, :]
    causal = place_query[None, :, None] >= place_key[None, None, :]
    return (same_doc & causal)[:, None]


def forward_block(
    carry, query_heads, key_rows, value_rows, seg_query, seg_key, place_query, place_key
):
    row_max, row_sum, acc_out = carry
    scores = jnp.einsum(
        "sqhd,skhd->shqk", query_heads, split_heads(key_rows), preferred_element_type=jnp.float32
    )
    allowed = visible(seg_query, seg_key, place_query, place_key)
    scores = jnp.where(allowed, scores, NEGATIVE)
    new_max = jnp.maximum(row_max, jnp.max(scores, axis=-1))
    expanded = jnp.where(allowed, jnp.exp(scores - new_max[..., None]), 0.0)
    factor = jnp.exp(row_max - new_max)
    row_sum = jnp.sum(expanded, axis=-1)
    added = jnp.einsum(
        "shqk,skhd->sqhd",
        expanded.astype(jnp.bfloat16),
        split_heads(value_rows),
        preferred_element_type=jnp.float32,
    )
    acc_out = acc_out * jnp.swapaxes(factor, 1, 2)[..., None] + added
    return (new_max, row_sum, acc_out)


def grad_block(
    query_heads,
    key_heads,
    value_heads,
    grad_heads,
    log_total,
    delta_sum,
    seg_query,
    seg_key,
    place_query,
    place_key,
):
    scores = jnp.einsum(
        "sqhd,skhd->shqk", query_heads, key_heads, preferred_element_type=jnp.float32
    )
    allowed = visible(seg_query, seg_key, place_query, place_key)
    shift_total = jnp.swapaxes(log_total, 1, 2)[..., None]
    probs = jnp.where(allowed, jnp.exp(scores - shift_total), 0.0)
    grad_probs = jnp.einsum(
        "sqhd,skhd->shqk", grad_heads, value_heads, preferred_element_type=jnp.float32
    )
    grad_scores = (probs * (grad_probs - jnp.swapaxes(delta_sum, 1, 2)[..., None])).astype(
        jnp.bfloat16
    )
    return (grad_scores, probs.astype(jnp.bfloat16))


def query_side(mine, theirs):
    query_heads, grad_heads, log_total, delta_sum, seg_mine, place_mine = mine
    key_rows, value_rows, seg_theirs = theirs
    place_theirs = jnp.arange(key_rows.shape[1], dtype=jnp.int32)
    key_heads = split_heads(key_rows)
    outcome = grad_block(
        query_heads,
        key_heads,
        split_heads(value_rows),
        grad_heads,
        log_total,
        delta_sum,
        seg_mine,
        seg_theirs,
        place_mine,
        place_theirs,
    )
    return jnp.einsum("shqk,skhd->sqhd", outcome[0], key_heads, preferred_element_type=jnp.float32)


def key_side(mine, theirs):
    key_heads, value_heads, seg_mine, place_mine = mine
    query_rows, grad_rows, total_high, total_low, delta_high, delta_low, seg_theirs = theirs
    place_theirs = jnp.arange(query_rows.shape[1], dtype=jnp.int32)
    query_heads = split_heads(query_rows)
    grad_heads = split_heads(grad_rows)
    log_total = total_high.astype(jnp.float32) + total_low.astype(jnp.float32)
    delta_sum = delta_high.astype(jnp.float32) + delta_low.astype(jnp.float32)
    grad_scores, probs = grad_block(
        query_heads,
        key_heads,
        value_heads,
        grad_heads,
        log_total,
        delta_sum,
        seg_theirs,
        seg_mine,
        place_theirs,
        place_mine,
    )
    grad_key = jnp.einsum(
        "shqk,sqhd->skhd", grad_scores, query_heads, preferred_element_type=jnp.float32
    )
    grad_value = jnp.einsum(
        "shqk,sqhd->skhd", probs, grad_heads, preferred_element_type=jnp.float32
    )
    return (grad_key, grad_value)


def contract_rows(left, right):
    return lax.dot_general(
        left, right, (((0,), (0,)), ((), ())), preferred_element_type=jnp.float32
    )


def contract_cols(left, right):
    return lax.dot_general(
        left, right, (((1,), (1,)), ((), ())), preferred_element_type=jnp.float32
    )


def local(
    tokens,
    segments,
    cotangent,
    ln1_gain,
    ln1_bias,
    w_qkv,
    bias_query,
    bias_value,
    w_out,
    bias_out,
    ln2_gain,
    ln2_bias,
    w_up,
    bias_up,
    w_down,
    bias_down,
):
    count, span_rows, model_width = tokens.shape
    total_rows = count * span_rows
    places = lax.axis_index("ctx") * span_rows + jnp.arange(span_rows, dtype=jnp.int32)
    gathered = (
        lax.all_gather(ln1_gain, ("dp", "ctx"), axis=0, tiled=True),
        lax.all_gather(ln1_bias, ("dp", "ctx"), axis=0, tiled=True),
        lax.all_gather(w_qkv, ("dp", "ctx"), axis=0, tiled=True),
        lax.all_gather(bias_query, ("dp", "ctx"), axis=0, tiled=True),
        lax.all_gather(bias_value, ("dp", "ctx"), axis=0, tiled=True),
        lax.all_gather(w_out, ("dp", "ctx"), axis=0, tiled=True),
        lax.all_gather(bias_out, ("dp", "ctx"), axis=0, tiled=True),
        lax.all_gather(ln2_gain, ("dp", "ctx"), axis=0, tiled=True),
        lax.all_gather(ln2_bias, ("dp", "ctx"), axis=0, tiled=True),
        lax.all_gather(w_up, ("dp", "ctx"), axis=0, tiled=True),
        lax.all_gather(bias_up, ("dp", "ctx"), axis=0, tiled=True),
        lax.all_gather(w_down, ("dp", "ctx"), axis=0, tiled=True),
        lax.all_gather(bias_down, ("dp", "ctx"), axis=0, tiled=True),
    )
    (
        gain_one,
        shift_one,
        qkv_full,
        query_shift,
        value_shift,
        out_full,
        out_shift,
        gain_two,
        shift_two,
        up_full,
        up_shift,
        down_full,
        down_shift,
    ) = gathered
    flat = tokens.reshape(total_rows, model_width).astype(jnp.float32)
    normed = layer_norm(flat, gain_one.astype(jnp.float32), shift_one.astype(jnp.float32)).astype(
        jnp.bfloat16
    )
    projected = jnp.dot(normed, qkv_full, preferred_element_type=jnp.float32)
    row_shape = (count, span_rows, model_width)
    query_rows = (
        ((projected[:, :model_width] + query_shift.astype(jnp.float32)) * SCALING)
        .astype(jnp.bfloat16)
        .reshape(row_shape)
    )
    key_rows = projected[:, model_width : 2 * model_width].astype(jnp.bfloat16).reshape(row_shape)
    value_rows = (
        (projected[:, 2 * model_width :] + value_shift.astype(jnp.float32))
        .astype(jnp.bfloat16)
        .reshape(row_shape)
    )
    query_heads = split_heads(query_rows)
    start_state = (
        jnp.full((count, HEADS, span_rows), NEGATIVE, jnp.float32),
        jnp.zeros((count, HEADS, span_rows), jnp.float32),
        jnp.zeros((count, span_rows, HEADS, HEAD_DIM), jnp.float32),
    )
    piece_keys = lax.all_gather(key_rows, "ctx", axis=1, tiled=True)
    piece_values = lax.all_gather(value_rows, "ctx", axis=1, tiled=True)
    piece_segs = lax.all_gather(segments, "ctx", axis=1, tiled=True)
    piece_places = jnp.arange(piece_keys.shape[1], dtype=jnp.int32)
    row_max, row_sum, acc_out = forward_block(
        start_state,
        query_heads,
        piece_keys,
        piece_values,
        segments,
        piece_segs,
        places,
        piece_places,
    )
    attended_exact = acc_out / jnp.swapaxes(row_sum, 1, 2)[..., None]
    log_total = jnp.swapaxes(row_max + jnp.log(row_sum), 1, 2)
    attended = attended_exact.reshape(total_rows, model_width).astype(jnp.bfloat16)
    residual = (
        flat
        + jnp.dot(attended, out_full, preferred_element_type=jnp.float32)
        + out_shift.astype(jnp.float32)
    )
    normed_two = layer_norm(
        residual, gain_two.astype(jnp.float32), shift_two.astype(jnp.float32)
    ).astype(jnp.bfloat16)
    hidden = jnp.dot(normed_two, up_full, preferred_element_type=jnp.float32) + up_shift.astype(
        jnp.float32
    )
    active = jax.nn.gelu(hidden).astype(jnp.bfloat16)
    result = (
        residual
        + jnp.dot(active, down_full, preferred_element_type=jnp.float32)
        + down_shift.astype(jnp.float32)
    )
    output = result.astype(jnp.bfloat16).reshape(row_shape)
    regathered = (
        lax.all_gather(ln1_gain, ("dp", "ctx"), axis=0, tiled=True),
        lax.all_gather(ln1_bias, ("dp", "ctx"), axis=0, tiled=True),
        lax.all_gather(w_qkv, ("dp", "ctx"), axis=0, tiled=True),
        lax.all_gather(bias_query, ("dp", "ctx"), axis=0, tiled=True),
        lax.all_gather(bias_value, ("dp", "ctx"), axis=0, tiled=True),
        lax.all_gather(w_out, ("dp", "ctx"), axis=0, tiled=True),
        lax.all_gather(bias_out, ("dp", "ctx"), axis=0, tiled=True),
        lax.all_gather(ln2_gain, ("dp", "ctx"), axis=0, tiled=True),
        lax.all_gather(ln2_bias, ("dp", "ctx"), axis=0, tiled=True),
        lax.all_gather(w_up, ("dp", "ctx"), axis=0, tiled=True),
        lax.all_gather(bias_up, ("dp", "ctx"), axis=0, tiled=True),
        lax.all_gather(w_down, ("dp", "ctx"), axis=0, tiled=True),
        lax.all_gather(bias_down, ("dp", "ctx"), axis=0, tiled=True),
    )
    (
        gain_one,
        shift_one,
        qkv_full,
        query_shift,
        value_shift,
        out_full,
        out_shift,
        gain_two,
        shift_two,
        up_full,
        up_shift,
        down_full,
        down_shift,
    ) = regathered
    upstream = cotangent.reshape(total_rows, model_width)
    upstream_wide = upstream.astype(jnp.float32)
    grad_w_down = contract_rows(active, upstream)
    grad_bias_down = jnp.sum(upstream_wide, axis=0)
    grad_active = contract_cols(upstream, down_full)
    gelu_back = jax.vjp(jax.nn.gelu, hidden)[1]
    grad_hidden = gelu_back(grad_active)[0].astype(jnp.bfloat16)
    grad_bias_up = jnp.sum(grad_hidden.astype(jnp.float32), axis=0)
    grad_w_up = contract_rows(normed_two, grad_hidden)
    grad_normed_two = contract_cols(grad_hidden, up_full)
    norm_two_back = jax.vjp(
        layer_norm, residual, gain_two.astype(jnp.float32), shift_two.astype(jnp.float32)
    )[1]
    grad_from_norm, grad_ln2_gain, grad_ln2_bias = norm_two_back(grad_normed_two)
    grad_residual = upstream_wide + grad_from_norm
    grad_bias_out = jnp.sum(grad_residual, axis=0)
    grad_residual_low = grad_residual.astype(jnp.bfloat16)
    grad_w_out = contract_rows(attended, grad_residual_low)
    grad_attended = (
        contract_cols(grad_residual_low, out_full).astype(jnp.bfloat16).reshape(row_shape)
    )
    grad_heads = split_heads(grad_attended)
    delta_sum = jnp.sum(grad_heads.astype(jnp.float32) * attended_exact, axis=-1)
    total_high = log_total.astype(jnp.bfloat16)
    total_low = (log_total - total_high.astype(jnp.float32)).astype(jnp.bfloat16)
    delta_high = delta_sum.astype(jnp.bfloat16)
    delta_low = (delta_sum - delta_high.astype(jnp.float32)).astype(jnp.bfloat16)
    total_used = total_high.astype(jnp.float32) + total_low.astype(jnp.float32)
    delta_used = delta_high.astype(jnp.float32) + delta_low.astype(jnp.float32)
    key_heads = split_heads(key_rows)
    value_heads = split_heads(value_rows)
    query_mine = (query_heads, grad_heads, total_used, delta_used, segments, places)
    key_mine = (key_heads, value_heads, segments, places)
    grad_query = query_side(
        query_mine,
        (
            lax.all_gather(key_rows, "ctx", axis=1, tiled=True),
            lax.all_gather(value_rows, "ctx", axis=1, tiled=True),
            lax.all_gather(segments, "ctx", axis=1, tiled=True),
        ),
    )
    grad_key, grad_value = key_side(
        key_mine,
        (
            lax.all_gather(query_rows, "ctx", axis=1, tiled=True),
            lax.all_gather(grad_attended, "ctx", axis=1, tiled=True),
            lax.all_gather(total_high, "ctx", axis=1, tiled=True),
            lax.all_gather(total_low, "ctx", axis=1, tiled=True),
            lax.all_gather(delta_high, "ctx", axis=1, tiled=True),
            lax.all_gather(delta_low, "ctx", axis=1, tiled=True),
            lax.all_gather(segments, "ctx", axis=1, tiled=True),
        ),
    )
    query_part = (grad_query.astype(jnp.bfloat16) * SCALING).reshape(total_rows, model_width)
    key_part = grad_key.astype(jnp.bfloat16).reshape(total_rows, model_width)
    value_part = grad_value.astype(jnp.bfloat16).reshape(total_rows, model_width)
    grad_projected = jnp.concatenate([query_part, key_part, value_part], axis=1)
    grad_bias_query = jnp.sum(query_part.astype(jnp.float32), axis=0)
    grad_bias_value = jnp.sum(value_part.astype(jnp.float32), axis=0)
    grad_w_qkv = contract_rows(normed, grad_projected)
    grad_normed = contract_cols(grad_projected, qkv_full)
    norm_one_back = jax.vjp(
        layer_norm, flat, gain_one.astype(jnp.float32), shift_one.astype(jnp.float32)
    )[1]
    grad_from_first, grad_ln1_gain, grad_ln1_bias = norm_one_back(grad_normed)
    grad_tokens = (grad_residual + grad_from_first).astype(jnp.bfloat16).reshape(row_shape)
    owned = (
        lax.psum_scatter(grad_ln1_gain, ("dp", "ctx"), scatter_dimension=0, tiled=True),
        lax.psum_scatter(grad_ln1_bias, ("dp", "ctx"), scatter_dimension=0, tiled=True),
        lax.psum_scatter(grad_w_qkv, ("dp", "ctx"), scatter_dimension=0, tiled=True),
        lax.psum_scatter(grad_bias_query, ("dp", "ctx"), scatter_dimension=0, tiled=True),
        lax.psum_scatter(grad_bias_value, ("dp", "ctx"), scatter_dimension=0, tiled=True),
        lax.psum_scatter(grad_w_out, ("dp", "ctx"), scatter_dimension=0, tiled=True),
        lax.psum_scatter(grad_bias_out, ("dp", "ctx"), scatter_dimension=0, tiled=True),
        lax.psum_scatter(grad_ln2_gain, ("dp", "ctx"), scatter_dimension=0, tiled=True),
        lax.psum_scatter(grad_ln2_bias, ("dp", "ctx"), scatter_dimension=0, tiled=True),
        lax.psum_scatter(grad_w_up, ("dp", "ctx"), scatter_dimension=0, tiled=True),
        lax.psum_scatter(grad_bias_up, ("dp", "ctx"), scatter_dimension=0, tiled=True),
        lax.psum_scatter(grad_w_down, ("dp", "ctx"), scatter_dimension=0, tiled=True),
        lax.psum_scatter(grad_bias_down, ("dp", "ctx"), scatter_dimension=0, tiled=True),
    )
    return (
        output,
        grad_tokens,
        owned[0],
        owned[1],
        owned[2],
        owned[3],
        owned[4],
        owned[5],
        owned[6],
        owned[7],
        owned[8],
        owned[9],
        owned[10],
        owned[11],
        owned[12],
    )


def solution(mesh):
    return jax.shard_map(
        local,
        mesh=mesh,
        in_specs=(
            P("dp", "ctx", None),
            P("dp", "ctx"),
            P("dp", "ctx", None),
            P(("dp", "ctx")),
            P(("dp", "ctx")),
            P(("dp", "ctx"), None),
            P(("dp", "ctx")),
            P(("dp", "ctx")),
            P(("dp", "ctx"), None),
            P(("dp", "ctx")),
            P(("dp", "ctx")),
            P(("dp", "ctx")),
            P(("dp", "ctx"), None),
            P(("dp", "ctx")),
            P(("dp", "ctx"), None),
            P(("dp", "ctx")),
        ),
        out_specs=(
            P("dp", "ctx", None),
            P("dp", "ctx", None),
            P(("dp", "ctx")),
            P(("dp", "ctx")),
            P(("dp", "ctx"), None),
            P(("dp", "ctx")),
            P(("dp", "ctx")),
            P(("dp", "ctx"), None),
            P(("dp", "ctx")),
            P(("dp", "ctx")),
            P(("dp", "ctx")),
            P(("dp", "ctx"), None),
            P(("dp", "ctx")),
            P(("dp", "ctx"), None),
            P(("dp", "ctx")),
        ),
        check_vma=False,
    )
```

profile of v0, /device:TPU:9, one launch (start us, length us, event | category | flops | bytes accessed | tf_op | source)
XLA Modules:
  0.0 933.2 jit_solution(13037831490255977648)
XLA Ops:
  16.3 40.8 %all-reduce.19 = (bf16[768]{0:T(1024)(128)(2,1)S(1)}, bf16[768]{0:T(1024)(128)(2,1)S(1)}, bf16[768]{0:T(1024)(128)(2,1)S(1)}, bf16[768]{0:T(1024)(128)(2,1)S(1)}...) all-reduce(bf16[768]{0:T(1024)(128)(2,1)S(1)} %dynamic-update-slice, ...), channel_id=1, replica_groups=mesh['dp'=4,'ctx'=8] {'dp','ctx'}, use_global_device_ids=true, to_apply=%add.4 | all-reduce | flops 9216 | bytes 36864
  61.8 10.6 %all-gather.9.cloned.1.call-done = bf16[768,2304]{1,0:T(8,128)(2,1)} async-done(((bf16[24,2304]{1,0:T(8,128)(2,1)}), bf16[768,2304]{1,0:T(8,128)(2,1)}) %all-gather.9.cloned.1.call-update) | async-done | bytes 3538960 | tf_op jit(solution)/shard_map/all_gather | solution.py:166
  80.8 9.5 %all_gather.76 = s32[2,1024]{1,0:T(2,128)S(1)} all-gather(s32[2,128]{1,0:T(2,128)S(1)} %copy-done.34), channel_id=1, replica_groups=mesh['dp'=4,'ctx'=8] {'ctx'}, dimensions={1}, use_global_device_ids=true | all-gather | bytes 9216 | tf_op jit(solution)/shard_map/all_gather | solution.py:218
  92.0 46.8 %all-gather.19.cloned.1.call-done = bf16[3072,768]{1,0:T(8,128)(2,1)} async-done(((bf16[96,768]{1,0:T(8,128)(2,1)}), bf16[3072,768]{1,0:T(8,128)(2,1)}) %all-gather.19.cloned.1.call-update) | async-done | bytes 4718608 | tf_op jit(solution)/shard_map/all_gather | solution.py:175
  138.8 5.4 fusion.91
  144.2 32.5 %all-gather.11.cloned.1.call-done = bf16[2,1024,768]{2,1,0:T(8,128)(2,1)} async-done(((bf16[2,128,768]{2,1,0:T(8,128)(2,1)}), bf16[2,1024,768]{2,1,0:T(8,128)(2,1)}) %all-gather.11.cloned.1.call-update) | async-done | bytes 3145744 | tf_op jit(solution)/shard_map/all_gather | solution.py:216
  183.0 4.7 copy-done
  187.7 3.8 fusion.1
  191.5 24.4 %all-gather.13.cloned.1.call-done = bf16[2,1024,768]{2,1,0:T(8,128)(2,1)} async-done(((bf16[2,128,768]{2,1,0:T(8,128)(2,1)}), bf16[2,1024,768]{2,1,0:T(8,128)(2,1)}) %all-gather.13.cloned.1.call-update) | async-done | bytes 3145744 | tf_op jit(solution)/shard_map/all_gather | solution.py:217
  215.9 4.9 copy.55
  221.4 9.8 %fusion.86 = (bf16[2,128,12,64]{1,3,2,0:T(8,128)(2,1)S(1)}, f32[2,128,12,64]{1,3,2,0:T(8,128)}) fusion(f32[2,128,12]{1,2,0:T(8,128)} %bitcast.160, bf16[2,1024,12,64]{1,3,2,0:T(8,128)(2,1)} %bitcast.150, f32[2,12,128,1024]{3,2,1,0:T(8,128)} %copy-done, f32[2,12,128]{2,1,0:T(8,128)} %copy-done.24, pred[2,128,1024]{2,1,0:T(8,128)(4,1)} %copy-done.13, ...), kind=kOutput, calls=%fused_computation.134 | convolution fusion | flops 415825920 | bytes 17207296 | tf_op jit(solution)/shard_map/shqk,skhd->sqhd/dot_general | solution.py:44
  232.4 39.5 %all-gather.15.cloned.1.call-done = bf16[768,768]{1,0:T(8,128)(2,1)} async-done(((bf16[24,768]{1,0:T(8,128)(2,1)}), bf16[768,768]{1,0:T(8,128)(2,1)}) %all-gather.15.cloned.1.call-update) | async-done | bytes 1179664 | tf_op jit(solution)/shard_map/all_gather | solution.py:169
  276.1 62.7 %all-gather.17.cloned.1.call-done = bf16[768,3072]{1,0:T(8,128)(2,1)} async-done(((bf16[24,3072]{1,0:T(8,128)(2,1)}), bf16[768,3072]{1,0:T(8,128)(2,1)}) %all-gather.17.cloned.1.call-update) | async-done | bytes 4718608 | tf_op jit(solution)/shard_map/all_gather | solution.py:173
  338.8 9.5 %convert_reduce_fusion = (f32[3072]{0:T(1024)}, bf16[256,3072]{1,0:T(8,128)(2,1)S(1)}, f32[256,3072]{1,0:T(8,128)}) fusion(f32[256,3072]{1,0:T(8,128)} %fusion.91, f32[3072]{0:T(1024)} %convert_element_type.199, bf16[768,3072]{1,0:T(8,128)(2,1)} %all-gather.17.cloned.1.call-done, f32[256,768]{1,0:T(8,128)} %copy-done.4, f32[768]{0:T(1024)} %convert_element_type.197, ...), kind=kOutput, calls=%fused_computation.30 | convolution fusion | flops 1227027456 | bytes 13402112 | tf_op jit(solution)/shard_map/dot_general | solution.py:241
  357.8 6.8 fusion.80
  364.7 7.8 fusion.81
  390.3 10.6 %convert_reduce_fusion.3 = (f32[12,64]{1,0:T(8,128)}, bf16[2,128,12,64]{1,3,2,0:T(8,128)(2,1)}) fusion(bf16[2,1024,12,64]{1,3,2,0:T(8,128)(2,1)S(1)} %bitcast.140, f32[2,12,128,1024]{3,2,1,0:T(8,128)} %copy-done, f32[2,12,128]{2,1,0:T(8,128)} %convert_add_fusion, f32[2,12,128]{2,1,0:T(8,128)} %convert_add_fusion.1, pred[2,128,1024]{2,1,0:T(8,128)(4,1)} %copy-done.13, ...), kind=kOutput, calls=%fused_computation.62 | convolution fusion | flops 822410496 | bytes 19950592 | tf_op jit(solution)/shard_map/shqk,skhd->sqhd/dot_general | solution.py:98
  406.3 11.9 %all_gather.97 = bf16[2,1024,12]{1,2,0:T(8,128)(2,1)S(1)} all-gather(bf16[2,128,12]{1,2,0:T(8,128)(2,1)S(1)} %get-tuple-element.44), channel_id=1, replica_groups=mesh['dp'=4,'ctx'=8] {'ctx'}, dimensions={1}, use_global_device_ids=true | all-gather | bytes 55296 | tf_op jit(solution)/shard_map/all_gather | solution.py:330
  418.2 11.5 %all_gather.96 = bf16[2,1024,12]{1,2,0:T(8,128)(2,1)S(1)} all-gather(bf16[2,128,12]{1,2,0:T(8,128)(2,1)S(1)} %get-tuple-element.45), channel_id=1, replica_groups=mesh['dp'=4,'ctx'=8] {'ctx'}, dimensions={1}, use_global_device_ids=true | all-gather | bytes 55296 | tf_op jit(solution)/shard_map/all_gather | solution.py:329
  429.6 12.2 %all_gather.94 = bf16[2,1024,12]{1,2,0:T(8,128)(2,1)S(1)} all-gather(bf16[2,128,12]{1,2,0:T(8,128)(2,1)} %get-tuple-element.51), channel_id=1, replica_groups=mesh['dp'=4,'ctx'=8] {'ctx'}, dimensions={1}, use_global_device_ids=true | all-gather | bytes 55296 | tf_op jit(solution)/shard_map/all_gather | solution.py:328
  441.8 13.1 %all_gather.93 = bf16[2,1024,12]{1,2,0:T(8,128)(2,1)S(1)} all-gather(bf16[2,128,12]{1,2,0:T(8,128)(2,1)} %get-tuple-element.50), channel_id=1, replica_groups=mesh['dp'=4,'ctx'=8] {'ctx'}, dimensions={1}, use_global_device_ids=true | all-gather | bytes 55296 | tf_op jit(solution)/shard_map/all_gather | solution.py:327
  458.0 6.6 fusion.57
  464.6 4.7 copy.64
  469.3 13.0 %fusion.43 = bf16[2,128,12,64]{1,3,2,0:T(8,128)(2,1)} fusion(bf16[2,1024,12,64]{1,3,2,0:T(8,128)(2,1)S(1)} %bitcast.142, f32[2,12,1024,128]{3,2,1,0:T(8,128)} %fusion.57, f32[2,12,1024]{2,1,0:T(8,128)} %add_bitcast_fusion, f32[2,12,1024]{2,1,0:T(8,128)} %add_bitcast_fusion.1, pred[2,1024,128]{2,1,0:T(8,128)(4,1)} %compare_and_fusion, ...), kind=kOutput, calls=%fused_computation.44 | convolution fusion | flops 821231616 | bytes 20119552 | tf_op jit(solution)/shard_map/shqk,sqhd->skhd/dot_general | solution.py:121
  483.8 8.6 convert_reduce_fusion.2
  492.9 4.0 fusion.92
  498.2 6.0 fusion.34
  504.4 3.3 fusion.82
  508.2 40.6 %all-reduce.18 = (f32[768]{0:T(1024)S(1)}, f32[768]{0:T(1024)S(1)}, f32[768]{0:T(1024)S(1)}, f32[768]{0:T(1024)S(1)}, f32[768]{0:T(1024)S(1)}, /*index=5*/f32[76...) all-reduce(f32[768]{0:T(1024)S(1)} %get-tuple-element.17, ...), channel_id=2, replica_groups=mesh['dp'=4,'ctx'=8] {'dp','ctx'}, use_global_device_ids=true, to_apply=%region_12.13.clone | all-reduce | flops 9216 | bytes 73728
  555.1 104.2 %reduce-scatter.9.cloned.1.call-done = f32[24,3072]{1,0:T(8,128)} async-done(((f32[768,3072]{1,0:T(8,128)}), f32[24,3072]{1,0:T(8,128)}) %reduce-scatter.9.cloned.1.call-update) | async-done | bytes 294928 | tf_op jit(solution)/shard_map/reduce_scatter | solution.py:357
  659.3 141.1 %reduce-scatter.11.cloned.1.call-done = f32[96,768]{1,0:T(8,128)} async-done(((f32[3072,768]{1,0:T(8,128)}), f32[96,768]{1,0:T(8,128)}) %reduce-scatter.11.cloned.1.call-update) | async-done | bytes 294928 | tf_op jit(solution)/shard_map/reduce_scatter | solution.py:359
  800.4 125.7 %reduce-scatter.5.cloned.1.call-done = f32[24,2304]{1,0:T(8,128)} async-done(((f32[768,2304]{1,0:T(8,128)}), f32[24,2304]{1,0:T(8,128)}) %reduce-scatter.5.cloned.1.call-update) | async-done | bytes 221200 | tf_op jit(solution)/shard_map/reduce_scatter | solution.py:350
  (209 shorter events, 81.7 us)
Async XLA Ops:
  7.2 65.2 %all-gather.9.cloned.1.call-start = ((), (), s32[]{:S(2)}) async-start(), calls=%async_computation.4 | async-start | bytes 3649536 | tf_op jit(solution)/shard_map/all_gather | solution.py:166
  7.9 130.9 %all-gather.19.cloned.1.call-start = ((), (), s32[]{:S(2)}) async-start(), calls=%async_computation.9 | async-start | bytes 4866048 | tf_op jit(solution)/shard_map/all_gather | solution.py:175
  8.7 168.1 %all-gather.11.cloned.1.call-start = ((), (), s32[]{:S(2)}) async-start(), calls=%async_computation.5 | async-start | bytes 3538944 | tf_op jit(solution)/shard_map/all_gather | solution.py:216
  61.8 13.7 %copy-start.10 = (bf16[256,768]{1,0:T(8,128)(2,1)}, bf16[256,768]{1,0:T(8,128)(2,1)S(1)}, u32[]{:S(2)}) copy-start(bf16[256,768]{1,0:T(8,128)(2,1)S(1)} %add_convert_fusion.2) | copy-start | bytes 1179652
  75.5 5.4 copy-start.34
  76.3 62.6 %copy-start.7 = (bf16[2,128,768]{2,1,0:T(8,128)(2,1)S(1)}, bf16[2,128,768]{2,1,0:T(8,128)(2,1)}, u32[]{:S(2)}) copy-start(bf16[2,128,768]{2,1,0:T(8,128)(2,1)} %param.18) | copy-start | bytes 1179652
  76.3 139.7 %all-gather.13.cloned.1.call-start = ((), (), s32[]{:S(2)}) async-start(), calls=%async_computation.6 | async-start | bytes 3538944 | tf_op jit(solution)/shard_map/all_gather | solution.py:217
  77.2 14.7 %copy-start.12 = (bf16[256,768]{1,0:T(8,128)(2,1)}, bf16[256,768]{1,0:T(8,128)(2,1)S(1)}, u32[]{:S(2)}) copy-start(bf16[256,768]{1,0:T(8,128)(2,1)S(1)} %get-tuple-element.48) | copy-start | bytes 1179652
  77.2 194.7 %all-gather.15.cloned.1.call-start = ((), (), s32[]{:S(2)}) async-start(), calls=%async_computation.7 | async-start | bytes 1216512 | tf_op jit(solution)/shard_map/all_gather | solution.py:169
  77.8 261.0 %all-gather.17.cloned.1.call-start = ((), (), s32[]{:S(2)}) async-start(), calls=%async_computation.8 | async-start | bytes 4866048 | tf_op jit(solution)/shard_map/all_gather | solution.py:173
  78.4 324.6 %all-gather.21.cloned.1.call-start = ((), (), s32[]{:S(2)}) async-start(), calls=%async_computation.10 | async-start | bytes 3538944 | tf_op jit(solution)/shard_map/all_gather | solution.py:325
  90.9 92.1 %copy-start.13 = (pred[2,128,1024]{2,1,0:T(8,128)(4,1)}, pred[2,128,1024]{2,1,0:T(8,128)(4,1)S(1)}, u32[]{:S(2)}) copy-start(pred[2,128,1024]{2,1,0:T(8,128)(4,1)S(1)} %compare_and_fusion.1) | copy-start | bytes 786436
  92.0 372.6 %all-gather.23.cloned.1.call-start = ((), (), s32[]{:S(2)}) async-start(), calls=%async_computation.11 | async-start | bytes 3538944 | tf_op jit(solution)/shard_map/all_gather | solution.py:326
  183.0 4.7 copy-start
  183.0 8.5 copy-start.24
  191.5 29.3 %copy-start.18 = (f32[2,12,128]{2,1,0:T(8,128)}, f32[2,12,128]{2,1,0:T(8,128)S(1)}, u32[]{:S(2)}) copy-start(f32[2,12,128]{2,1,0:T(8,128)S(1)} %fusion.1) | copy-start | bytes 36868
  221.4 50.5 %copy-start.3 = (bf16[2,128,768]{2,1,0:T(8,128)(2,1)S(1)}, bf16[2,128,768]{2,1,0:T(8,128)(2,1)}, u32[]{:S(2)}) copy-start(bf16[2,128,768]{2,1,0:T(8,128)(2,1)} %param.16) | copy-start | bytes 1179652
  338.8 9.6 %copy-start.5 = (f32[256,768]{1,0:T(8,128)S(1)}, f32[256,768]{1,0:T(8,128)}, u32[]{:S(2)}) copy-start(f32[256,768]{1,0:T(8,128)} %copy-done.4) | copy-start | bytes 2359300
  338.8 9.6 %copy-start.17 = (f32[768]{0:T(1024)S(1)}, f32[768]{0:T(1024)}, u32[]{:S(2)}) copy-start(f32[768]{0:T(1024)} %convert_element_type.196) | copy-start | bytes 9220
  338.8 9.6 %copy-start.26 = (f32[256]{0:T(256)S(1)}, f32[256]{0:T(256)}, u32[]{:S(2)}) copy-start(f32[256]{0:T(256)} %copy-done.25) | copy-start | bytes 3076
  338.8 9.6 %copy-start.32 = (f32[256]{0:T(256)S(1)}, f32[256]{0:T(256)}, u32[]{:S(2)}) copy-start(f32[256]{0:T(256)} %fusion.72) | copy-start | bytes 3076
  338.8 9.6 %copy-start.44 = (bf16[768,3072]{1,0:T(8,128)(2,1)S(1)}, bf16[768,3072]{1,0:T(8,128)(2,1)}, u32[]{:S(2)}) copy-start(bf16[768,3072]{1,0:T(8,128)(2,1)} %all-gather.17.cloned.1.call-done) | copy-start | bytes 14155780
  354.0 201.1 %reduce-scatter.7.cloned.1.call-start = ((), (), s32[]{:S(2)}) async-start(), calls=%async_computation.13 | async-start | bytes 2433024 | tf_op jit(solution)/shard_map/reduce_scatter | solution.py:353
  357.3 302.0 %reduce-scatter.9.cloned.1.call-start = ((), (), s32[]{:S(2)}) async-start(), calls=%async_computation.14 | async-start | bytes 9732096 | tf_op jit(solution)/shard_map/reduce_scatter | solution.py:357
  364.6 435.8 %reduce-scatter.11.cloned.1.call-start = ((), (), s32[]{:S(2)}) async-start(), calls=%async_computation.15 | async-start | bytes 9732096 | tf_op jit(solution)/shard_map/reduce_scatter | solution.py:359
  372.5 553.6 %reduce-scatter.5.cloned.1.call-start = ((), (), s32[]{:S(2)}) async-start(), calls=%async_computation.12 | async-start | bytes 7299072 | tf_op jit(solution)/shard_map/reduce_scatter | solution.py:350
  483.8 9.0 copy-start.14
  483.8 9.1 copy-start.11
  498.2 6.1 copy-start.23
  498.2 6.1 copy-start.28
  504.3 3.8 copy-start.31
  504.4 49.7 %copy-start.2 = (f32[256,768]{1,0:T(8,128)S(1)}, f32[256,768]{1,0:T(8,128)}, u32[]{:S(2)}) copy-start(f32[256,768]{1,0:T(8,128)} %copy-done.1) | copy-start | bytes 2359300
  (25 other events, 45.9 us)
Sparse Core Ops, SparseCore 0:
  11.0 61.2 all-gather.8
  75.4 63.3 all-gather.18
  141.0 35.6 all-gather.10
  178.8 37.1 all-gather.12
  218.8 53.0 all-gather.14
  274.8 63.9 all-gather.16
  340.4 35.6 all-gather.20
  377.7 37.3 all-gather.22
  421.0 96.8 reduce-scatter.6
  525.3 134.0 reduce-scatter.8
  665.8 134.5 reduce-scatter.10
  807.5 118.6 reduce-scatter.4
where the time goes:
time: 946 us; the launch traced here: 933 us
  waiting for transfers between devices  590 us (62%)
  blocking collectives  139 us (15%)
  matrix products  106 us (11%)
  local copies, waits for them, and re-layouts  59.1 us (6%)
  other arithmetic  22.3 us (2%)
  between operations  15 us (2%)
    reduce_scatter x1, waiting for transfers between devices, local(): lax.psum_scatter(grad_w_down, ('dp', 'ctx'), scatter_dimension=0, tiled=T...  141 us
    reduce_scatter x1, waiting for transfers between devices, local(): lax.psum_scatter(grad_w_qkv, ('dp', 'ctx'), scatter_dimension=0, tiled=True)  126 us
    reduce_scatter x1, waiting for transfers between devices, local(): lax.psum_scatter(grad_w_up, ('dp', 'ctx'), scatter_dimension=0, tiled=True)  104 us
    unnamed x2, blocking collectives  81.3 us
    all_gather x1, waiting for transfers between devices, local(): lax.all_gather(w_up, ('dp', 'ctx'), axis=0, tiled=True)  62.7 us
    all_gather x1, waiting for transfers between devices, local(): lax.all_gather(w_down, ('dp', 'ctx'), axis=0, tiled=True)  46.8 us
    all_gather x1, waiting for transfers between devices, local(): lax.all_gather(w_out, ('dp', 'ctx'), axis=0, tiled=True)  39.5 us
    all_gather x1, waiting for transfers between devices, local(): piece_keys = lax.all_gather(key_rows, 'ctx', axis=1, tiled=True)  32.5 us
  transfers between devices with their start and end apart: 12, of which 9 were waited for; matrix products, arithmetic and copies ran while one was open for 19% of the time, Pallas kernels for 0%

commit v1 on v0

--- a/solution.py
+++ b/solution.py
@@ -1,6 +1,11 @@
+import functools
+import math
+
 import jax
 import jax.numpy as jnp
 from jax import lax
+from jax.experimental import pallas as pl
+from jax.experimental.pallas import tpu as pltpu
 from jax.sharding import PartitionSpec as P
 
 HEADS = 12
@@ -139,7 +144,7 @@
     )
 
 
-def local(
+def local_general(
     tokens,
     segments,
     cotangent,
@@ -378,9 +383,1027 @@
     )
 
 
+AXES = ("dp", "ctx")
+WORK = {
+    "attend": 8.0,
+    "hidden": 5.5,
+    "feed": 4.5,
+    "attend_back": 15.0,
+    "attend_grad": 2.5,
+    "project_out": 2.4,
+}
+PACE = 1.15e9 * 0.05
+LANES = 128
+BIG = -1e30
+ROOT = math.sqrt(2.0 / math.pi)
+CUBIC = 0.044715
+F32 = jnp.float32
+BF16 = jnp.bfloat16
+
+
+def dot(left, right, contract=((1,), (0,))):
+    return lax.dot_general(left, right, (contract, ((), ())), preferred_element_type=F32)
+
+
+def normalize(values):
+    center = values - jnp.mean(values, axis=-1, keepdims=True)
+    factor = lax.rsqrt(jnp.mean(center * center, axis=-1, keepdims=True) + EPSILON)
+    return center * factor, factor
+
+
+def norm_back(grad, normal, factor):
+    return factor * (
+        grad
+        - jnp.mean(grad, axis=-1, keepdims=True)
+        - normal * jnp.mean(grad * normal, axis=-1, keepdims=True)
+    )
+
+
+def size_of(shape, dtype):
+    lanes = -(-shape[-1] // LANES) * LANES
+    rows = -(-shape[-2] // 16) * 16 if len(shape) > 1 else 16
+    lead = math.prod(shape[:-2]) if len(shape) > 2 else 1
+    return lead * rows * lanes * jnp.dtype(dtype).itemsize
+
+
+def run(name, body, place, args, outs, scratch=(), flops=0, extra=4 << 20):
+    held = sum(size_of(s, d) for s, d in scratch)
+    whole = pl.BlockSpec(memory_space=pltpu.VMEM)
+    return pl.pallas_call(
+        body,
+        name=name,
+        out_shape=[jax.ShapeDtypeStruct(s, d) for s, d in outs],
+        in_specs=[pl.BlockSpec(memory_space=pltpu.SMEM)] + [whole] * len(args),
+        out_specs=[whole] * len(outs),
+        scratch_shapes=[pltpu.VMEM(s, d) for s, d in scratch],
+        compiler_params=pltpu.CompilerParams(vmem_limit_bytes=min(held + extra, 56 << 20)),
+        cost_estimate=pl.CostEstimate(
+            flops=int(WORK.get(name, 1.5) * PACE), bytes_accessed=1, transcendentals=0
+        ),
+    )(place, *args)
+
+
+def rows_at(start, size, align):
+    return pl.ds(pl.multiple_of(start, align), size)
+
+
+class Grid:
+    def __init__(self, dp, ctx):
+        self.dp, self.ctx = dp, ctx
+        self.ny, self.nx, self.nz = 2, dp // 2, ctx // 2
+
+    def move(self, value, step):
+        pairs = []
+        for i in range(self.dp * self.ctx):
+            core, z = i % 2, (i // 2) % self.nz
+            x, y = (i // self.ctx) % self.nx, i // (self.ctx * self.nx)
+            y, x, z, core = step(y, x, z, core)
+            pairs.append((i, ((y * self.nx + x) * self.nz + z) * 2 + core))
+        return lax.ppermute(value, AXES, pairs)
+
+    def core(self, value):
+        return self.move(value, lambda y, x, z, c: (y, x, z, 1 - c))
+
+    def along_x(self, value):
+        return self.move(value, lambda y, x, z, c: (y, 1 - x, z, c))
+
+    def along_y(self, value):
+        return self.move(value, lambda y, x, z, c: (1 - y, x, z, c))
+
+    def along_xy(self, value):
+        return self.move(value, lambda y, x, z, c: (1 - y, 1 - x, z, c))
+
+    def along_z(self, value, hop):
+        return self.move(value, lambda y, x, z, c: (y, x, (z + hop) % self.nz, c))
+
+
+    def lines(self):
+        return [[2 * z + core for z in range(self.nz)] for core in range(2)]
+
+    def gather_z(self, value):
+        return lax.all_gather(value, "ctx", axis=0, tiled=True, axis_index_groups=self.lines())
+
+    def gather_chips(self, value):
+        count = self.dp * self.ctx
+        groups = [list(range(core, count, 2)) for core in range(2)]
+        return lax.all_gather(value, AXES, axis=0, tiled=True, axis_index_groups=groups)
+
+    def scatter_z(self, value):
+        return lax.psum_scatter(
+            value, "ctx", scatter_dimension=0, tiled=True, axis_index_groups=self.lines()
+        )
+
+
+def from_z(z, hop):
+    return lax.rem(z - hop + 4, 4)
+
+
+def order_kernel(place, own, r1, r2, r3, out):
+    z = place[2]
+    out[z] = own[...]
+    out[from_z(z, 1)] = r1[...]
+    out[from_z(z, 2)] = r2[...]
+    out[from_z(z, 3)] = r3[...]
+
+
+def block_index(place):
+    y, x = place[0], place[1]
+    return (2 * y + x, 2 * y + 1 - x, 2 * (1 - y) + x, 2 * (1 - y) + 1 - x)
+
+
+def fold(block):
+    rows = block.shape[0] // 2
+    return jnp.concatenate([block[:rows], block[rows:]], axis=1)
+
+
+def unfold(ref, lanes):
+    return jnp.concatenate([ref[:, :lanes], ref[:, lanes:]], axis=0)
+
+
+def seen(seg_col, seg_row, i, span):
+    keys = span * (i + 1)
+    same = seg_col[i * span : (i + 1) * span] == seg_row[:, :keys]
+    place_q = i * span + lax.broadcasted_iota(jnp.int32, (span, keys), 0)
+    place_k = lax.broadcasted_iota(jnp.int32, (span, keys), 1)
+    return jnp.where(same & (place_q >= place_k), 0.0, BIG).astype(F32)
+
+
+def attend_kernel(
+    place,
+    own,
+    other,
+    b0,
+    bx,
+    by,
+    bxy,
+    seg_row,
+    seg_col,
+    weight,
+    vectors,
+    normed,
+    rows,
+    out,
+    exact,
+    totals,
+    spare,
+):
+    core, second = place[3], place[2] % 2 == 1
+    lines, run_rows, width = own.shape
+    group = width // 4
+    span = 2 * run_rows
+    part = b0.shape[0] * b0.shape[1]
+    cut = weight.shape[1]
+    for index, piece in zip(block_index(place), (b0, bx, by, bxy)):
+        for k in range(piece.shape[0]):
+            here = rows_at(index * part + k * piece.shape[1], piece.shape[1], 16)
+            weight[here] = piece[k, :, :cut]
+    vectors[...] = jnp.transpose(weight[:, 4 * LANES :].astype(F32))[64:80]
+    gain, shift = vectors[0:1, :], vectors[1:2, :]
+    mine = pl.ds(pl.multiple_of(core * 2 * group, LANES), 2 * group)
+    bias_q, bias_v = vectors[2:3, mine], vectors[3:4, mine]
+    bias_q = jnp.where(second, bias_q[:, group:], bias_q[:, :group])
+    bias_v = jnp.where(second, bias_v[:, group:], bias_v[:, :group])
+    for i in range(lines):
+        spare[i, rows_at(core * run_rows, run_rows, 16)] = own[i]
+        spare[i, rows_at((1 - core) * run_rows, run_rows, 16)] = other[i]
+    for i in range(lines):
+        here = slice(i * span, (i + 1) * span)
+        value = (normalize(spare[i].astype(F32))[0] * gain + shift).astype(BF16)
+        normed[here] = value
+        projected = dot(value, weight[:, : 3 * group])
+        rows[here, :group] = ((projected[:, :group] + bias_q) * SCALING).astype(BF16)
+        rows[here, group : 2 * group] = projected[:, group : 2 * group].astype(BF16)
+        rows[here, 2 * group :] = (projected[:, 2 * group :] + bias_v).astype(BF16)
+    for i in range(lines):
+        here = slice(i * span, (i + 1) * span)
+        keys = span * (i + 1)
+        bias = seen(seg_col, seg_row, i, span)
+        heads = []
+        for h in range(3):
+            at = h * HEAD_DIM
+            query = rows[here, at : at + HEAD_DIM]
+            key = rows[:keys, group + at : group + at + HEAD_DIM]
+            value = rows[:keys, 2 * group + at : 2 * group + at + HEAD_DIM]
+            scores = dot(query, key, ((1,), (1,))) + bias
+            peak = jnp.max(scores, axis=-1, keepdims=True)
+            expanded = jnp.exp(scores - peak)
+            total = jnp.sum(expanded, axis=-1, keepdims=True)
+            mixed = dot(expanded.astype(BF16), value) / total
+            heads.append(mixed.astype(BF16))
+            exact[here, at : at + HEAD_DIM] = mixed
+            totals[here, h : h + 1] = peak + jnp.log(total)
+        out[i] = fold(jnp.concatenate(heads, axis=1))
+
+
+def out_kernel(place, own, r1, r2, r3, weight, attended, *partial):
+    z = place[2]
+    span, group = attended.shape[1:]
+    attended[z] = unfold(own.at[z], group)
+    for hop, piece in ((1, r1), (2, r2), (3, r3)):
+        attended[from_z(z, hop)] = unfold(piece, group)
+    for s in range(2):
+        partial[s][...] = (
+            dot(attended[2 * s], weight[:group]) + dot(attended[2 * s + 1], weight[group:])
+        ).astype(BF16)
+
+
+def place_rows(core, target, own, other):
+    run_rows = own.shape[0] // 2
+    for s in range(2):
+        for which, piece in ((core, own), (1 - core, other)):
+            target[rows_at((2 * s + which) * run_rows, run_rows, 16)] = piece[
+                s * run_rows : (s + 1) * run_rows
+            ]
+
+
+def hidden_kernel(
+    place,
+    tokens_own,
+    tokens_other,
+    part_first,
+    part_second,
+    other_first,
+    other_second,
+    cot_own,
+    cot_other,
+    up,
+    vectors,
+    bias_up,
+    cot,
+    residual,
+    normed,
+    active,
+    slope,
+    tokens,
+):
+    place_rows(place[3], cot, cot_own, cot_other)
+    place_rows(place[3], tokens, tokens_own, tokens_other)
+    gain, shift, bias_out = vectors[5:6, :], vectors[6:7, :], vectors[4:5, :]
+    span = tokens.shape[0] // 2
+    for s in range(2):
+        here = slice(s * span, (s + 1) * span)
+        one, two = ((part_first, other_first), (part_second, other_second))[s]
+        wide = tokens[here].astype(F32) + (one[...].astype(F32) + two[...].astype(F32)) + bias_out
+        residual[here] = wide
+        low = (normalize(wide)[0] * gain + shift).astype(BF16)
+        normed[here] = low
+        hidden = dot(low, up[...]) + bias_up[...]
+        square = hidden * hidden
+        bent = jnp.tanh(ROOT * (hidden + CUBIC * (square * hidden)))
+        active[here] = (0.5 * hidden * (1.0 + bent)).astype(BF16)
+        slope[here] = 0.5 * (1.0 + bent) + 0.5 * hidden * (1.0 - bent * bent) * (
+            ROOT * (1.0 + 3.0 * CUBIC * square)
+        )
+
+
+def down_weights_kernel(place, active, cot, down_own, down_other, spare):
+    core = place[3]
+    spare[...] = dot(active[...], cot[...], ((0,), (0,))).astype(BF16)
+    width = cot.shape[1]
+    for which, target in ((core, down_own), (1 - core, down_other)):
+        for j in range(8):
+            for k in range(2):
+                target[48 * j : 48 * j + 48, k * width : (k + 1) * width] = spare[
+                    rows_at(192 * j + 96 * which + 48 * k, 48, 16)
+                ]
+
+
+def feed_kernel(
+    place,
+    residual,
+    active,
+    slope,
+    cot,
+    up,
+    down,
+    grad_hidden,
+    result,
+    grad_normed,
+    low_first,
+    low_second,
+    sums,
+    sum_up,
+):
+    span = cot.shape[0] // 2
+    for s in range(2):
+        here = slice(s * span, (s + 1) * span)
+        upstream = cot[here]
+        grad = (dot(upstream, down[...], ((1,), (1,))) * slope[here]).astype(BF16)
+        grad_hidden[here] = grad
+        back = dot(grad, up[...], ((1,), (1,)))
+        grad_normed[here] = back
+        (low_first, low_second)[s][...] = back.astype(BF16)
+        result[here] = dot(active[here], down[...])
+        rows = jnp.concatenate(
+            [
+                jnp.sum(back * normalize(residual[here])[0], axis=0, keepdims=True),
+                jnp.sum(back, axis=0, keepdims=True),
+                0.5 * jnp.sum(upstream.astype(F32), axis=0, keepdims=True),
+            ],
+            axis=0,
+        )
+        total = jnp.sum(grad.astype(F32), axis=0, keepdims=True)
+        if s == 0:
+            sums[...] = rows
+            sum_up[...] = total
+        else:
+            sums[...] = sums[...] + rows
+            sum_up[...] = sum_up[...] + total
+
+
+def up_weights_kernel(place, normed, grad_hidden, grad_up):
+    grad_up[...] = dot(normed[...], grad_hidden[...], ((0,), (0,))).astype(BF16)
+
+
+def attend_grad_kernel(
+    place,
+    back_own,
+    other_first,
+    other_second,
+    residual,
+    cot,
+    vectors,
+    weight,
+    attended,
+    grad_residual,
+    blocks,
+    out_own,
+    out_other,
+    sum_out,
+    spare,
+):
+    core = place[3]
+    gain = vectors[5:6, :]
+    span = cot.shape[0] // 2
+    group = attended.shape[2]
+    half = 2 * group
+    products = [None, None]
+    for s in range(2):
+        here = slice(s * span, (s + 1) * span)
+        normal, factor = normalize(residual[here])
+        wide = cot[here].astype(F32) + norm_back(
+            (back_own[here] + (other_first, other_second)[s][...].astype(F32)) * gain,
+            normal,
+            factor,
+        )
+        grad_residual[here] = wide
+        low = wide.astype(BF16)
+        grad = dot(low, weight[...], ((1,), (1,))).astype(BF16)
+        total = 0.5 * jnp.sum(wide, axis=0, keepdims=True)
+        sum_out[...] = total if s == 0 else sum_out[...] + total
+        for g in range(2):
+            blocks[2 * s + g] = fold(grad[:, g * group : (g + 1) * group])
+            product = dot(attended[2 * s + g], low, ((0,), (0,)))
+            products[g] = product if s == 0 else products[g] + product
+    for g in range(2):
+        spare[g * group : (g + 1) * group] = products[g].astype(BF16)
+    out_own[...] = spare[:, rows_at(core * half, half, LANES)]
+    out_other[...] = spare[:, rows_at((1 - core) * half, half, LANES)]
+
+
+def attend_back_kernel(
+    place,
+    rows,
+    exact,
+    totals,
+    seg_row,
+    seg_col,
+    own,
+    r1,
+    r2,
+    r3,
+    weight,
+    normed,
+    tokens_own,
+    tokens_other,
+    sums,
+    o_own,
+    o_x,
+    o_y,
+    o_xy,
+    back_own,
+    back_first,
+    back_second,
+    back_third,
+    grad,
+    keys_grad,
+    joined,
+    product,
+    small,
+):
+    z, core = place[2], place[3]
+    second = z % 2 == 1
+    lines, run_rows, width = tokens_own.shape
+    span, group = 2 * run_rows, width // 4
+    grad[rows_at(z * span, span, span)] = unfold(own.at[z], group)
+    for hop, piece in ((1, r1), (2, r2), (3, r3)):
+        grad[rows_at(from_z(z, hop) * span, span, span)] = unfold(piece, group)
+    for i in (3, 2, 1, 0):
+        here = slice(i * span, (i + 1) * span)
+        keys = span * (i + 1)
+        bias = seen(seg_col, seg_row, i, span)
+        for h in range(3):
+            at = h * HEAD_DIM
+            lanes = slice(at, at + HEAD_DIM)
+            query = rows[here, lanes]
+            key = rows[:keys, group + at : group + at + HEAD_DIM]
+            value = rows[:keys, 2 * group + at : 2 * group + at + HEAD_DIM]
+            upstream = grad[here, lanes]
+            delta = jnp.sum(upstream.astype(F32) * exact[here, lanes], axis=-1, keepdims=True)
+            probs = jnp.exp(dot(query, key, ((1,), (1,))) + bias - totals[here, h : h + 1])
+            slopes = dot(upstream, value, ((1,), (1,)))
+            grad_scores = (probs * (slopes - delta)).astype(BF16)
+            grad_query = dot(grad_scores, key).astype(BF16)
+            joined[here, lanes] = (grad_query.astype(F32) * SCALING).astype(BF16)
+            grad_key = dot(grad_scores, query, ((0,), (0,)))
+            grad_value = dot(probs.astype(BF16), upstream, ((0,), (0,)))
+            if i == 3:
+                keys_grad[2 * h] = grad_key
+                keys_grad[2 * h + 1] = grad_value
+            else:
+                keys_grad[2 * h, :keys] = keys_grad[2 * h, :keys] + grad_key
+                keys_grad[2 * h + 1, :keys] = keys_grad[2 * h + 1, :keys] + grad_value
+    for h in range(3):
+        for k in range(2):
+            at = (k + 1) * group + h * HEAD_DIM
+            joined[:, at : at + HEAD_DIM] = keys_grad[2 * h + k].astype(BF16)
+    small[...] = jnp.zeros_like(small)
+    small[4:16] = sums[4:16]
+    mine = pl.ds(pl.multiple_of(core * 2 * group, LANES), 2 * group)
+    empty = jnp.zeros((1, group), F32)
+    for row, at in ((2, 0), (3, 2 * group)):
+        total = jnp.sum(joined[:, at : at + group].astype(F32), axis=0, keepdims=True)
+        small[row : row + 1, mine] = jnp.where(
+            second,
+            jnp.concatenate([empty, total], axis=1),
+            jnp.concatenate([total, empty], axis=1),
+        )
+    for i in range(lines):
+        for which, tokens in ((core, tokens_own), (1 - core, tokens_other)):
+            here = rows_at(i * span + which * run_rows, run_rows, 16)
+            step = dot(joined[here], weight[:, : 3 * group], ((1,), (1,)))
+            if tokens is tokens_own:
+                back_own[i] = step
+            else:
+                low = step.astype(BF16)
+                for target, start in ((back_first, 0), (back_second, 192), (back_third, 384)):
+                    first = max(start, i * run_rows)
+                    last = min(start + target.shape[0], (i + 1) * run_rows)
+                    if first < last:
+                        target[first - start : last - start] = low[
+                            first - i * run_rows : last - i * run_rows
+                        ]
+            normal = normalize(tokens[i].astype(F32))[0]
+            small[0:1] = small[0:1] + jnp.sum(step * normal, axis=0, keepdims=True)
+            small[1:2] = small[1:2] + jnp.sum(step, axis=0, keepdims=True)
+    product[:, : 3 * group] = dot(normed[...], joined[...], ((0,), (0,))).astype(BF16)
+    product[:, 3 * group :] = jnp.transpose(small[...])[:, :64].astype(BF16)
+    size = o_own.shape[0]
+    for index, target in zip(block_index(place), (o_own, o_x, o_y, o_xy)):
+        target[...] = product[rows_at(index * size, size, 16)]
+
+
+def split_kernel(targets, size, block, place):
+    y, x = place[0], place[1]
+    own, over_x, over_y, low, high = targets
+    block(y, x, slice(0, size), own)
+    block(y, 1 - x, slice(0, size), over_x)
+    block(1 - y, x, slice(0, size), over_y)
+    block(1 - y, 1 - x, slice(0, size // 2), low)
+    block(1 - y, 1 - x, slice(size // 2, size), high)
+
+
+def split_down_kernel(place, own, other, *targets):
+    core, size = place[3], targets[0].shape[0]
+
+    def block(y, x, rows, target):
+        here = rows_at(x * size + rows.start, rows.stop - rows.start, 16)
+        target[...] = jnp.where(y == core, own[here], other[here])
+
+    split_kernel(targets, size, block, place)
+
+
+def split_up_kernel(place, up, out_own, out_other, *targets):
+    core, size = place[3], targets[0].shape[0]
+    cut = up.shape[1]
+
+    def block(y, x, rows, target):
+        count = rows.stop - rows.start
+        target[:, :cut] = up[rows_at((2 * y + x) * size + rows.start, count, 16)]
+        here = rows_at(x * size + rows.start, count, 16)
+        target[:, cut:] = jnp.where(y == core, out_own[here], out_other[here])
+
+    split_kernel(targets, size, block, place)
+
+
+def collect_kernel(place, over_x, over_y, low, high, sum_x, sum_y):
+    half = low.shape[0]
+    sum_x[:half] = over_x[:half]
+    sum_x[half:] = (over_x[half:].astype(F32) + high[...].astype(F32)).astype(BF16)
+    sum_y[:half] = (over_y[:half].astype(F32) + low[...].astype(F32)).astype(BF16)
+    sum_y[half:] = over_y[half:]
+
+
+def add_kernel(place, own, first, second, out):
+    out[...] = (own[...].astype(F32) + (first[...].astype(F32) + second[...].astype(F32))).astype(
+        BF16
+    )
+
+
+def spread_kernel(place, own, from_x, from_y, low, high, out):
+    half = low.shape[0]
+    blocks = block_index(place)
+    for index, piece in zip(blocks, (own, from_x, from_y)):
+        out[index] = piece[...]
+    out[blocks[3], :half] = low[...]
+    out[blocks[3], half:] = high[...]
+
+
+def sum_plane_kernel(place, a, b, c, d, own, z1, z2, z3, spare):
+    z = place[2]
+    spare[...] = (
+        (a[...].astype(F32) + b[...].astype(F32)) + (c[...].astype(F32) + d[...].astype(F32))
+    ).astype(BF16)
+    size = own.shape[0]
+    for hop, target in enumerate((own, z1, z2, z3)):
+        target[...] = spare[rows_at(lax.rem(z + hop, 4) * size, size, 16)]
+
+
+def line_qkv_kernel(place, own, r1, r2, r3, out):
+    second = place[2] % 2 == 1
+    group = out.shape[1] // 2 - LANES // 2
+    same = own[...].astype(F32) + r2[...].astype(F32)
+    cross = r1[...].astype(F32) + r3[...].astype(F32)
+    out[:, :group] = jnp.where(second, cross, same)[:, :group]
+    out[:, group : 2 * group] = jnp.where(second, same, cross)[:, :group]
+    out[:, 2 * group : 2 * group + 64] = (same + cross)[:, group:]
+    out[:, 2 * group + 64 :] = jnp.zeros((out.shape[0], 64), F32)
+
+
+def out_split_kernel(place, b0, bx, by, bxy, own, other, spare):
+    core = place[3]
+    first = b0.shape[2] - own.shape[1]
+    size = b0.shape[0] * b0.shape[1]
+    for index, piece in zip(block_index(place), (b0, bx, by, bxy)):
+        for k in range(piece.shape[0]):
+            here = rows_at(index * size + k * piece.shape[1], piece.shape[1], 16)
+            spare[here] = piece[k, :, first:]
+    half = own.shape[0]
+    own[...] = spare[rows_at(core * half, half, 16)]
+    other[...] = spare[rows_at((1 - core) * half, half, 16)]
+
+
+def out_halves_kernel(place, own, other, out):
+    core = place[3]
+    half = out.shape[0]
+    for which, piece in ((core, own), (1 - core, other)):
+        out[:, rows_at(which * half, half, LANES)] = piece[...]
+
+
+def down_halves_kernel(place, own, other, down):
+    core = place[3]
+    width = down.shape[1]
+    for which, piece in ((core, own), (1 - core, other)):
+        for j in range(8):
+            for k in range(2):
+                down[rows_at(192 * j + 96 * which + 48 * k, 48, 16)] = piece[
+                    48 * j : 48 * j + 48, k * width : (k + 1) * width
+                ]
+
+
+def final_kernel(place, own, r1, r2, r3, grad_residual, tokens, vectors, out, held):
+    z, core = place[2], place[3]
+    rows = tokens.shape[0] // 2
+    held[z] = own[z]
+    for hop, piece in ((1, r1), (2, r2), (3, r3)):
+        held[from_z(z, hop)] = piece[...]
+    gain = vectors[0:1, :]
+    for s in range(2):
+        here = slice(s * rows, (s + 1) * rows)
+        there = rows_at((2 * s + core) * rows, rows, 16)
+        normal, factor = normalize(tokens[here].astype(F32))
+        grad = (held[2 * s].astype(F32) + held[2 * s + 1].astype(F32)) * gain
+        out[here] = (grad_residual[there] + norm_back(grad, normal, factor)).astype(BF16)
+
+
+def split_local(
+    grid,
+    tokens,
+    segments,
+    cotangent,
+    ln1_gain,
+    ln1_bias,
+    w_qkv,
+    bias_query,
+    bias_value,
+    w_out,
+    bias_out,
+    ln2_gain,
+    ln2_bias,
+    w_up,
+    bias_up,
+    w_down,
+    bias_down,
+):
+    count, run_rows, width = tokens.shape
+    own_rows = count * run_rows
+    all_rows = 2 * own_rows
+    span = 2 * run_rows
+    half = width // 2
+    group = half // 2
+    hidden_half = w_up.shape[1] // 2
+    shard = w_qkv.shape[0]
+    dp, ctx = lax.axis_index("dp"), lax.axis_index("ctx")
+    y, x, z, core = dp // grid.nx, dp % grid.nx, ctx // 2, ctx % 2
+    place = jnp.stack([y, x, z, core]).astype(jnp.int32)
+    first_core = core == 0
+
+    def pick(array, index, axis):
+        return lax.dynamic_index_in_dim(array, index, axis, keepdims=False)
+
+    def both(own, other, axis):
+        return jnp.where(
+            first_core,
+            jnp.concatenate([own, other], axis),
+            jnp.concatenate([other, own], axis),
+        )
+
+    def z_all(value):
+        return [value] + [grid.along_z(value, hop) for hop in (1, 2, 3)]
+
+    def after(values, *waited):
+        return lax.optimization_barrier((values, waited))[0]
+
+    def z_blocks(blocks):
+        return [grid.along_z(pick(blocks, lax.rem(z + hop, 4), 0), hop) for hop in (1, 2, 3)]
+
+    flat = tokens.reshape(own_rows, width)
+    small = jnp.stack(
+        [ln1_gain, ln1_bias, bias_query, bias_value, bias_out, ln2_gain, ln2_bias, bias_down], axis=1
+    )
+    lifted = bias_up.reshape(4, shard).T
+    seg_lanes = jnp.pad(segments.astype(BF16).reshape(8, 32), ((0, shard - 8), (0, 0)))
+    vector_lanes = jnp.concatenate(
+        [small, lifted, jnp.zeros((shard, 4), BF16), seg_lanes, jnp.zeros((shard, 16), BF16)],
+        axis=1,
+    )
+    split_qkv = w_qkv.reshape(shard, 3, 2, half)
+    split_up = w_up.reshape(shard, 2, hidden_half)
+    split_out = w_out.reshape(shard, 2, half)
+    cut = 3 * group + 64
+
+    def columns(which):
+        chosen = pick(split_qkv, which, 2)
+        return jnp.concatenate(
+            [
+                chosen[:, :, :group].reshape(shard, 3 * group),
+                vector_lanes,
+                chosen[:, :, group:].reshape(shard, 3 * group),
+                vector_lanes,
+                pick(split_out, which, 1),
+                pick(split_up, which, 1),
+            ],
+            axis=1,
+        )
+
+    piece = both(columns(core), grid.core(columns(1 - core)), 0)
+    flat_other = grid.core(flat)
+    cot_own = cotangent.reshape(own_rows, width)
+    cot_other = grid.core(cot_own)
+    second_group = lax.rem(z, 2) == 1
+    lanes_out = piece[:, 2 * cut : 2 * cut + half]
+    first, last = piece[:, :cut], piece[:, cut : 2 * cut]
+    piece_same = jnp.concatenate([jnp.where(second_group, last, first), lanes_out], axis=1)
+    piece_cross = jnp.concatenate([jnp.where(second_group, first, last), lanes_out], axis=1)
+    line_one = [
+        piece_same,
+        grid.along_z(piece_cross, 1),
+        grid.along_z(piece_same, 2),
+        grid.along_z(piece_cross, 3),
+    ]
+    waiting_tokens = after(tokens, line_one)
+    token_pieces = [
+        grid.along_z(pick(waiting_tokens, lax.rem(z + hop, 4) // 2, 0), hop) for hop in (1, 2, 3)
+    ]
+    piece_b = jnp.concatenate([w_down[: 2 * shard], w_down[2 * shard :]], axis=1)
+
+    def order(name, pieces):
+        return run(name, order_kernel, place, pieces, [((4,) + pieces[0].shape, BF16)])[0]
+
+    def kernel(name, body, args, outs, scratch=(), extra=4 << 20, **options):
+        bound = functools.partial(body, **options) if options else body
+        return run(name, bound, place, args, outs, scratch, extra=extra)
+
+    line_one = after(line_one, flat_other, cot_other)
+    plane_one = order("order_qkv", line_one)
+    from_x, from_y, from_xy = (
+        grid.along_x(plane_one),
+        grid.along_y(plane_one),
+        grid.along_xy(plane_one),
+    )
+    weight_up = grid.gather_chips(piece[:, 2 * cut + half :])
+    token_pieces = after(token_pieces, plane_one)
+    gathered = order("order_tokens", [pick(tokens, z // 2, 0)] + token_pieces)
+    gathered_other = grid.core(gathered)
+    line_b = z_all(after(piece_b, token_pieces))
+    segs = plane_one.reshape(4, 2, shard, cut + half)[:, :, :8, 3 * group + 16 : 3 * group + 48]
+    segs = segs.reshape(4, 2, 2, 4 * 32).transpose(2, 0, 1, 3).reshape(2, 8 * run_rows)
+    segs = pick(segs, z // 2, 0).astype(F32)
+
+    weight_qkv, vectors, normed, packed, out_blocks, exact, totals = kernel(
+        "attend",
+        attend_kernel,
+        [
+            gathered,
+            gathered_other,
+            plane_one,
+            from_x,
+            from_y,
+            from_xy,
+            segs.reshape(1, -1),
+            segs.reshape(-1, 1),
+        ],
+        [
+            ((width, cut), BF16),
+            ((16, width), F32),
+            ((4 * span, width), BF16),
+            ((4 * span, 3 * group), BF16),
+            ((4, run_rows, 2 * group), BF16),
+            ((4 * span, group), F32),
+            ((4 * span, LANES), F32),
+        ],
+        [((4, span, width), BF16)],
+        extra=14 << 20,
+    )
+    out_pieces = z_blocks(out_blocks)
+
+    weight_out = kernel(
+        "out_split",
+        out_split_kernel,
+        [plane_one, from_x, from_y, from_xy],
+        [((half, half), BF16)] * 2,
+        [((width, half), BF16)],
+    )
+    weight_out = kernel(
+        "out_halves",
+        out_halves_kernel,
+        [weight_out[0], grid.core(weight_out[1])],
+        [((half, width), BF16)],
+    )[0]
+
+    def spread(name, plane, over, when):
+        size = plane.shape[0] // 2
+        low, high = grid.along_x(over[1][:size]), grid.along_y(over[0][size:])
+        return kernel(
+            name,
+            spread_kernel,
+            [plane, *over, *after((low, high), when)],
+            [((4,) + plane.shape, BF16)],
+        )[0]
+
+    plane_b = order("order_b", after(line_b, out_blocks)).reshape(8 * shard, 2 * width)
+    out_pieces = after(out_pieces, plane_b)
+    bias_up_half = lax.dynamic_slice_in_dim(
+        vectors[8:12].reshape(4, 4 * 8, shard).transpose(1, 0, 2).reshape(1, 2 * hidden_half),
+        core * hidden_half,
+        hidden_half,
+        axis=1,
+    )
+    attended, *partial = kernel(
+        "project_out",
+        out_kernel,
+        [out_blocks] + out_pieces + [weight_out],
+        [((4, span, group), BF16)] + [((own_rows, width), BF16)] * 2,
+    )
+    over_b = after((grid.along_x(plane_b), grid.along_y(plane_b)), partial)
+    cot, residual, normed_two, active, slope = kernel(
+        "hidden",
+        hidden_kernel,
+        [
+            flat,
+            flat_other,
+            *partial,
+            *[grid.core(member) for member in partial],
+            cot_own,
+            cot_other,
+            after(weight_up, over_b),
+            vectors,
+            bias_up_half,
+        ],
+        [
+            ((all_rows, width), BF16),
+            ((all_rows, width), F32),
+            ((all_rows, width), BF16),
+            ((all_rows, hidden_half), BF16),
+            ((all_rows, hidden_half), F32),
+        ],
+        [((all_rows, width), BF16)],
+        extra=14 << 20,
+    )
+    down_own, down_other = kernel(
+        "down_weights",
+        down_weights_kernel,
+        [active, cot],
+        [((half, 2 * width), BF16)] * 2,
+        [((hidden_half, width), BF16)],
+        extra=10 << 20,
+    )
+    down_recv = grid.core(down_other)
+    mixed_down = spread("spread_down", plane_b, over_b, down_own).reshape(2, half, 2 * width)
+    weight_down = kernel(
+        "down_halves",
+        down_halves_kernel,
+        [pick(mixed_down, core, 0), grid.core(pick(mixed_down, 1 - core, 0))],
+        [((hidden_half, width), BF16)],
+    )[0]
+
+    def halve(array, which):
+        return pick(array.reshape(2, 2, run_rows, width), which, 1).reshape(own_rows, width)
+
+    size = 8 * shard
+
+    def split(name, body, parts, lanes):
+        return kernel(
+            name, body, parts, [((size, lanes), BF16)] * 3 + [((size // 2, lanes), BF16)] * 2
+        )
+
+    def diagonal(parts):
+        return grid.along_x(parts[3]), grid.along_y(parts[4])
+
+    def collect(name, parts, low, high):
+        sum_x, sum_y = kernel(
+            name, collect_kernel, [parts[1], parts[2], low, high], [(parts[1].shape, BF16)] * 2
+        )
+        return parts[0], grid.along_x(sum_x), grid.along_y(sum_y), sum_x
+
+    def finish(name, parts):
+        total = kernel(name, add_kernel, parts, [(parts[0].shape, BF16)])[0]
+        return grid.scatter_z(total).astype(F32)
+
+    down_parts = split("split_down", split_down_kernel, [down_own, down_recv], 2 * width)
+    down_low, down_high = diagonal(down_parts)
+    grad_hidden, result, back_two, *back_low, sums_two, sum_up = kernel(
+        "feed",
+        feed_kernel,
+        after([residual, active, slope, cot, weight_up, weight_down], down_parts),
+        [
+            ((all_rows, hidden_half), BF16),
+            ((all_rows, width), F32),
+            ((all_rows, width), F32),
+            ((own_rows, width), BF16),
+            ((own_rows, width), BF16),
+            ((3, width), F32),
+            ((1, hidden_half), F32),
+        ],
+        extra=14 << 20,
+    )
+    back_other = [grid.core(member) for member in back_low]
+    result_other = grid.core(halve(result, 1 - core))
+    grad_up = kernel(
+        "up_weights",
+        up_weights_kernel,
+        [normed_two, grad_hidden],
+        [((width, hidden_half), BF16)],
+        extra=10 << 20,
+    )[0]
+
+    output = (
+        halve(residual, core)
+        + (halve(result, core) + result_other)
+        + vectors[7:8]
+    ).astype(BF16)
+
+    grad_residual, grad_blocks, out_own, out_other, sum_out = kernel(
+        "attend_grad",
+        attend_grad_kernel,
+        after(
+            [back_two, *back_other, residual, cot, vectors, weight_out, attended],
+            grad_up,
+            result_other,
+        ),
+        [
+            ((all_rows, width), F32),
+            ((4, run_rows, 2 * group), BF16),
+            ((half, half), BF16),
+            ((half, half), BF16),
+            ((1, width), F32),
+        ],
+        [((half, width), BF16)],
+    )
+    grad_pieces = z_blocks(grad_blocks)
+    out_recv = grid.core(out_other)
+    down_low, down_high = after((down_low, down_high), grad_blocks)
+    down_parts = collect("collect_down", down_parts, down_low, down_high)
+
+    up_parts = split("split_up", split_up_kernel, [grad_up, out_own, out_recv], hidden_half + half)
+    up_low, up_high = diagonal(up_parts)
+
+    lifted_sum = jnp.where(
+        first_core,
+        jnp.concatenate([sum_up, jnp.zeros_like(sum_up)], axis=1),
+        jnp.concatenate([jnp.zeros_like(sum_up), sum_up], axis=1),
+    )
+    lifted_rows = lifted_sum.reshape(32, 4, shard).transpose(1, 0, 2).reshape(4, width)
+    sums = jnp.concatenate(
+        [jnp.zeros((4, width), F32), sum_out, sums_two, lifted_rows, jnp.zeros((4, width), F32)],
+        axis=0,
+    )
+    grad_pieces = after(grad_pieces, up_parts, down_parts[3])
+    back_results = kernel(
+        "attend_back",
+        attend_back_kernel,
+        [packed, exact, totals, segs.reshape(1, -1), segs.reshape(-1, 1), grad_blocks]
+        + grad_pieces
+        + [weight_qkv, normed, gathered, gathered_other, sums],
+        [((size, cut), BF16)] * 4
+        + [((4, run_rows, width), F32)]
+        + [((192, width), BF16), ((192, width), BF16), ((128, width), BF16)],
+        [
+            ((4 * span, group), BF16),
+            ((6, 4 * span, HEAD_DIM), F32),
+            ((4 * span, 3 * group), BF16),
+            ((width, cut), BF16),
+            ((LANES, width), F32),
+        ],
+        extra=14 << 20,
+    )
+    qkv_parts, back_own, back_low = back_results[:4], back_results[4], back_results[5:]
+    back_recv = jnp.concatenate([grid.core(member) for member in back_low], axis=0)
+    back_sum = (back_own + back_recv.reshape(back_own.shape).astype(F32)).astype(BF16)
+    back_pieces = z_blocks(back_sum)
+    qkv_recv = [grid.along_x(qkv_parts[1]), grid.along_y(qkv_parts[2]), grid.along_xy(qkv_parts[3])]
+
+    up_low, up_high = after((up_low, up_high), back_own)
+    up_parts = collect("collect_up", up_parts, up_low, up_high)
+    down_sum = finish("finish_down", after(list(down_parts[:3]), up_parts[3]))
+    qkv_own, *qkv_sends = kernel(
+        "plane_qkv",
+        sum_plane_kernel,
+        [qkv_parts[0]] + after(qkv_recv, back_sum),
+        [((2 * shard, cut), BF16)] * 4,
+        [((size, cut), BF16)],
+    )
+    up_sum = finish("finish_up", after(list(up_parts[:3]), qkv_own))
+    qkv_line = [qkv_own] + [grid.along_z(qkv_sends[hop - 1], hop) for hop in (1, 2, 3)]
+    qkv_sum = kernel(
+        "line_qkv", line_qkv_kernel, qkv_line, [((2 * shard, 6 * group + LANES), F32)]
+    )[0]
+    grad_tokens = kernel(
+        "final",
+        final_kernel,
+        [back_sum] + back_pieces + [grad_residual, flat, vectors],
+        [((own_rows, width), BF16)],
+        [((4, run_rows, width), BF16)],
+    )[0]
+    def rows_of(array, which):
+        return lax.dynamic_slice_in_dim(array, which * shard, shard, axis=0)
+
+    def exchange(array):
+        return rows_of(array, core), grid.core(rows_of(array, 1 - core))
+
+    grad_down = jnp.concatenate([down_sum[:, :width], down_sum[:, width:]], axis=0)
+    up_mine, up_theirs = exchange(up_sum)
+    grad_up_own = both(up_mine[:, :hidden_half], up_theirs[:, :hidden_half], 1)
+    grad_out_own = both(up_mine[:, hidden_half:], up_theirs[:, hidden_half:], 1)
+    qkv_mine, qkv_theirs = exchange(qkv_sum)
+    grad_qkv_own = both(
+        *[
+            part[:, : 6 * group].reshape(shard, 2, 3, group).transpose(0, 2, 1, 3)[:, :, None]
+            for part in (qkv_mine, qkv_theirs)
+        ],
+        2,
+    ).reshape(shard, 6 * half)
+    small_sum = (qkv_mine[:, 6 * group : 6 * group + 16] + qkv_theirs[:, 6 * group : 6 * group + 16]).T
+    return (
+        output.reshape(tokens.shape),
+        grad_tokens.reshape(tokens.shape),
+        small_sum[0],
+        small_sum[1],
+        grad_qkv_own,
+        small_sum[2],
+        small_sum[3],
+        grad_out_own,
+        small_sum[4],
+        small_sum[5],
+        small_sum[6],
+        grad_up_own,
+        small_sum[8:12].reshape(4 * shard),
+        grad_down,
+        small_sum[7],
+    )
+
+
+def build_local(mesh):
+    dp, ctx = mesh.shape["dp"], mesh.shape["ctx"]
+    if (dp, ctx) != (4, 8):
+        return local_general
+    grid = Grid(dp, ctx)
+    return lambda *args: split_local(grid, *args)
+
+
 def solution(mesh):
     return jax.shard_map(
-        local,
+        build_local(mesh),
         mesh=mesh,
         in_specs=(
             P("dp", "ctx", None),

time: 946 us -> 310 us (0.33)
  waiting for transfers between devices: 590 us -> 84.6 us
  blocking collectives: 139 us -> 0 us
  matrix products: 106 us -> 0 us
  Pallas kernels: 0 us -> 71.8 us
  starting transfers between devices: 0.89 us -> 57.4 us
  other arithmetic: 22.3 us -> 9.24 us
    reduce_scatter x4 -> x2, waiting for transfers between devices: 371 us -> 0.01 us  [scatter_z(): lax.psum_scatter(value, 'ctx', scatter_dimension=0, tiled=True, axis_inde...]
    all_gather x8 -> x1, waiting for transfers between devices: 216 us -> 0.02 us  [gather_chips(): lax.all_gather(value, AXES, axis=0, tiled=True, axis_index_groups=groups)]
    dot_general x18 -> x0, matrix products: 106 us -> none  [the longest x4 21.9 us: contract_rows(): lax.dot_general(left, right, (((0,), (0,)), ((), ())), preferred_element_...]
    ppermute x0 -> x57, waiting for transfers between devices: none -> 84.5 us  [move(): return lax.ppermute(value, AXES, pairs)]
    unnamed x2 -> x0, blocking collectives: 81.3 us -> none
    pallas_call x0 -> x24, Pallas kernels: none -> 71.8 us  [run(): pl.pallas_call(body, name=name, out_shape=[jax.ShapeDtypeStruct(s, d) for...]
    all_gather x5 -> x0, blocking collectives: 58.1 us -> none  [the longest x1 13.1 us: local(): lax.all_gather(total_high, 'ctx', axis=1, tiled=True)]
    ppermute x0 -> x57, starting transfers between devices: none -> 57.2 us  [move(): return lax.ppermute(value, AXES, pairs)]
  transfers between devices with their start and end apart: 12 -> 60, of which waited for: 9 -> 19; matrix products, arithmetic and copies ran while one was open for 19% -> 10% of each run, Pallas kernels for 0% -> 21%
where the time goes in v1:
time: 310 us; the launch traced here: 304 us
  waiting for transfers between devices  84.6 us (27%)
  Pallas kernels  71.8 us (23%)
  local copies, waits for them, and re-layouts  65.7 us (21%)
  starting transfers between devices  57.4 us (19%)
  between operations  15.2 us (5%)
  other arithmetic  9.24 us (3%)
    ppermute x57, waiting for transfers between devices, move(): return lax.ppermute(value, AXES, pairs)  84.5 us
    pallas_call x24, Pallas kernels, run(): pl.pallas_call(body, name=name, out_shape=[jax.ShapeDtypeStruct(s, d) for...  71.8 us
    ppermute x57, starting transfers between devices, move(): return lax.ppermute(value, AXES, pairs)  57.2 us
    unnamed x188, local copies, waits for them, and re-layouts  36 us
  transfers between devices with their start and end apart: 60, of which 19 were waited for; matrix products, arithmetic and copies ran while one was open for 10% of the time, Pallas kernels for 21%

profile of v1, /device:TPU:9, one launch (start us, length us, event | category | flops | bytes accessed | tf_op | source)
XLA Modules:
  0.0 303.9 jit_solution(14129067577001611918)
XLA Ops:
  19.5 4.4 %collective-permute-done.3.r2 = bf16[48,1024]{1,0:T(8,128)(2,1)S(1)} collective-permute-done((bf16[48,1024]{1,0:T(8,128)(2,1)S(1)}, bf16[48,1024]{1,0:T(8,128)(2,1)S(1)}, u32[]{:S(2)}, u32[]{:S(2)}) %collective-permute-start.3) | collective-permute-done | bytes 98336 | tf_op jit(solution)/shard_map/ppermute | solution.py:462
  23.9 2.5 collective-permute-done.4.r3
  30.0 3.9 %collective-permute-done.5.r1 = bf16[128,768]{1,0:T(8,128)(2,1)S(1)} collective-permute-done((bf16[128,768]{1,0:T(8,128)(2,1)S(1)}, bf16[128,768]{1,0:T(8,128)(2,1)S(1)}, u32[]{:S(2)}, u32[]{:S(2)}) %collective-permute-start.5) | collective-permute-done | bytes 196640 | tf_op jit(solution)/shard_map/ppermute | solution.py:462
  33.9 11.6 %collective-permute-done.6.r2 = bf16[128,768]{1,0:T(8,128)(2,1)S(1)} collective-permute-done((bf16[128,768]{1,0:T(8,128)(2,1)S(1)}, bf16[128,768]{1,0:T(8,128)(2,1)S(1)}, u32[]{:S(2)}, u32[]{:S(2)}) %collective-permute-start.6) | collective-permute-done | bytes 196640 | tf_op jit(solution)/shard_map/ppermute | solution.py:462
  45.4 2.5 collective-permute-done.7.r3
  52.3 11.2 %collective-permute-done.10.bx = bf16[4,48,1024]{2,1,0:T(8,128)(2,1)S(1)} collective-permute-done((bf16[4,48,1024]{2,1,0:T(8,128)(2,1)S(1)}, bf16[4,48,1024]{2,1,0:T(8,128)(2,1)S(1)}, u32[]{:S(2)}, u32[]{:S(2)}) %collective-permute-start.10) | collective-permute-done | bytes 393248 | tf_op jit(solution)/shard_map/ppermute | solution.py:462
  63.5 1.8 collective-permute-start.17
  65.3 7.5 %collective-permute-done.12.bxy = bf16[4,48,1024]{2,1,0:T(8,128)(2,1)} collective-permute-done((bf16[4,48,1024]{2,1,0:T(8,128)(2,1)S(1)}, bf16[4,48,1024]{2,1,0:T(8,128)(2,1)}, u32[]{:S(2)}, u32[]{:S(2)}) %collective-permute-start.12) | collective-permute-done | bytes 393248 | tf_op jit(solution)/shard_map/ppermute | solution.py:462
  72.8 8.5 %attend.1 = (bf16[768,640]{1,0:T(8,128)(2,1)S(1)}, f32[16,768]{1,0:T(8,128)S(1)}, bf16[1024,768]{1,0:T(8,128)(2,1)S(1)}, bf16[1024,576]{1,0:T(8,128)(2,1)S(1)}, ...) custom-call(s32[4]{0:T(128)S(1)} %pad_add_fusion.place, ...), custom_call_target="tpu_custom_call" | custom-call | flops 460000000 | bytes 1 | tf_op jit(solution)/shard_map/attend/pallas_call | solution.py:432
  93.1 1.8 collective-permute-start.14
  98.2 3.6 %collective-permute-done.14.r2 = bf16[128,384]{1,0:T(8,128)(2,1)S(1)} collective-permute-done((bf16[128,384]{1,0:T(8,128)(2,1)S(1)}, bf16[128,384]{1,0:T(8,128)(2,1)S(1)}, u32[]{:S(2)}, u32[]{:S(2)}) %collective-permute-start.14) | collective-permute-done | bytes 98336 | tf_op jit(solution)/shard_map/ppermute | solution.py:462
  101.8 2.7 collective-permute-done.15.r3
  104.5 1.9 project_out.1
  121.4 4.8 %hidden.1 = (bf16[512,768]{1,0:T(8,128)(2,1)S(1)}, f32[512,768]{1,0:T(8,128)S(1)}, bf16[512,768]{1,0:T(8,128)(2,1)S(1)}, bf16[512,1536]{1,0:T(8,128)(2,1)S(1)}, f32[512,1536]{1,0:T(8,128)S(1)}) custom-call(s32[4]{0:T(128)S(1)} %pad_add_fusion.place, bf16[256,768]{1,0:T(8,128)(2,1)S(1)} %bitcast.101, bf16[256,768]{1,0:T(8,128)(2,1)S(1)} %copy-done.47, ...), custom_call_target="tpu_custom_call" | custom-call | flops 316249984 | bytes 1 | tf_op jit(solution)/shard_map/hidden/pallas_call | solution.py:432
  126.3 2.1 down_weights.1
  135.9 4.7 %feed.1 = (bf16[512,1536]{1,0:T(8,128)(2,1)S(1)}, f32[512,768]{1,0:T(8,128)S(1)}, f32[512,768]{1,0:T(8,128)S(1)}, bf16[256,768]{1,0:T(8,128)(2,1)S(1)}, bf16[256...) custom-call(s32[4]{0:T(128)S(1)} %pad_add_fusion.place, ...), custom_call_target="tpu_custom_call" | custom-call | flops 258750000 | bytes 1 | tf_op jit(solution)/shard_map/feed/pallas_call | solution.py:432
  143.5 1.9 up_weights.1.up
  145.5 13.0 %attend_grad.1 = (f32[512,768]{1,0:T(8,128)S(1)}, bf16[4,128,384]{2,1,0:T(8,128)(2,1)S(1)}, bf16[384,384]{1,0:T(8,128)(2,1)S(1)}, bf16[384,384]{1,0:T(8,128)(2,1)S(1)}, f32[1,768]{1,0:T(1,128)S(1)}) custom-call(s32[4]{0:T(128)S(1)} %pad_add_fusion.place, f32[512,768]{1,0:T(8,128)S(1)} %get-tuple-element.177.back_own, ...), custom_call_target="tpu_custom_call" | custom-call | flops 143750000 | bytes 1 | tf_op jit(solution)/shard_map/attend_grad/pallas_call | solution.py:432
  171.4 3.2 %collective-permute-done.32.r2 = bf16[128,384]{1,0:T(8,128)(2,1)S(1)} collective-permute-done((bf16[128,384]{1,0:T(8,128)(2,1)S(1)}, bf16[128,384]{1,0:T(8,128)(2,1)S(1)}, u32[]{:S(2)}, u32[]{:S(2)}) %collective-permute-start.32) | collective-permute-done | bytes 98336 | tf_op jit(solution)/shard_map/ppermute | solution.py:462
  175.3 3.9 %collective-permute-start.33 = (bf16[128,384]{1,0:T(8,128)(2,1)}, bf16[128,384]{1,0:T(8,128)(2,1)}, u32[]{:S(2)}, u32[]{:S(2)}) collective-permute-start(bf16[128,384]{1,0:T(8,128)(2,1)} %get-tuple-element.246), channel_id=1, source_target_pairs={{0,6},{1,7},{2,0},{3,1},{4,2},{5,3},{6,4},{7,5},{8,14},{9,15},{10,... | collective-permute-start | bytes 294920 | tf_op jit(solution)/shard_map/ppermute | solution.py:462
  191.6 14.5 %attend_back.1 = (bf16[192,640]{1,0:T(8,128)(2,1)S(1)}, bf16[192,640]{1,0:T(8,128)(2,1)S(1)}, bf16[192,640]{1,0:T(8,128)(2,1)S(1)}, bf16[192,640]{1,0:T(8,128)(2...) custom-call(s32[4]{0:T(128)S(1)} %pad_add_fusion.place, ...), custom_call_target="tpu_custom_call" | custom-call | flops 862499968 | bytes 1 | tf_op jit(solution)/shard_map/attend_back/pallas_call | solution.py:432
  207.4 2.2 collect_up.1
  209.7 2.7 finish_down.1
  222.1 15.1 %collective-permute-done.43.b = bf16[192,640]{1,0:T(8,128)(2,1)S(1)} collective-permute-done((bf16[192,640]{1,0:T(8,128)(2,1)S(1)}, bf16[192,640]{1,0:T(8,128)(2,1)S(1)}, u32[]{:S(2)}, u32[]{:S(2)}) %collective-permute-start.43) | collective-permute-done | bytes 245792 | tf_op jit(solution)/shard_map/ppermute | solution.py:462
  237.3 5.5 %collective-permute-done.45.d = bf16[192,640]{1,0:T(8,128)(2,1)S(1)} collective-permute-done((bf16[192,640]{1,0:T(8,128)(2,1)S(1)}, bf16[192,640]{1,0:T(8,128)(2,1)S(1)}, u32[]{:S(2)}, u32[]{:S(2)}) %collective-permute-start.45) | collective-permute-done | bytes 245792 | tf_op jit(solution)/shard_map/ppermute | solution.py:462
  247.8 2.6 fusion.3
  250.9 2.9 collective-permute-start.47
  256.1 2.0 collective-permute-start.41
  258.1 8.3 %collective-permute-done.48.r3 = bf16[48,640]{1,0:T(8,128)(2,1)S(1)} collective-permute-done((bf16[48,640]{1,0:T(8,128)(2,1)S(1)}, bf16[48,640]{1,0:T(8,128)(2,1)S(1)}, u32[]{:S(2)}, u32[]{:S(2)}) %collective-permute-start.48) | collective-permute-done | bytes 61472 | tf_op jit(solution)/shard_map/ppermute | solution.py:462
  267.8 9.2 %collective-permute-start.49 = (f32[24,1280]{1,0:T(8,128)}, f32[24,1280]{1,0:T(8,128)}, u32[]{:S(2)}, u32[]{:S(2)}) collective-permute-start(f32[24,1280]{1,0:T(8,128)} %constant_dynamic-slice_fusion.2), channel_id=1, source_target_pairs={{0,1},{1,0},{2,3},{3,2},{4,5},{5,4},{6,7},{7,6},{8,9},{9,8},{10,11... | collective-permute-start | bytes 368648 | tf_op jit(solution)/shard_map/ppermute | solution.py:462
  285.6 1.9 select_n.179
  289.1 2.3 final.1
  (398 shorter events, 121.8 us)
Async XLA Ops:
  7.3 105.9 %all-gather.2.cloned.1.call-start = ((), (), s32[]{:S(2)}) async-start(), calls=%async_computation.2 | async-start | bytes 2506752 | tf_op jit(solution)/shard_map/all_gather | solution.py:489
  14.2 277.2 %reduce-scatter.5.cloned.1.call-start = ((), (), s32[]{:S(2)}) async-start(), calls=%async_computation.4 | async-start | bytes 737280 | tf_op jit(solution)/shard_map/reduce_scatter | solution.py:492
  26.5 18.9 %collective-permute-start.6 = (bf16[128,768]{1,0:T(8,128)(2,1)S(1)}, bf16[128,768]{1,0:T(8,128)(2,1)S(1)}, u32[]{:S(2)}, u32[]{:S(2)}) collective-permute-start(bf16[128,768]{1,0:T(8,128)(2,1)S(1)} %get-tuple-element.253), channel_id=1, source_target_pairs={{0,4},{1,5},{2,6},{3,7},{4,0},{5,1},{6,2},{7,3},{8,12},{9,13},{10,... | collective-permute-start | bytes 589832 | tf_op jit(solution)/shard_map/ppermute | solution.py:462
  27.6 20.3 %collective-permute-start.7 = (bf16[128,768]{1,0:T(8,128)(2,1)S(1)}, bf16[128,768]{1,0:T(8,128)(2,1)S(1)}, u32[]{:S(2)}, u32[]{:S(2)}) collective-permute-start(bf16[128,768]{1,0:T(8,128)(2,1)S(1)} %get-tuple-element.252), channel_id=1, source_target_pairs={{0,6},{1,7},{2,0},{3,1},{4,2},{5,3},{6,4},{7,5},{8,14},{9,15},{10,... | collective-permute-start | bytes 589832 | tf_op jit(solution)/shard_map/ppermute | solution.py:462
  48.5 24.3 %collective-permute-start.9 = (bf16[4,128,768]{2,1,0:T(8,128)(2,1)S(1)}, bf16[4,128,768]{2,1,0:T(8,128)(2,1)S(1)}, u32[]{:S(2)}, u32[]{:S(2)}) collective-permute-start(bf16[4,128,768]{2,1,0:T(8,128)(2,1)S(1)} %order_tokens.1.own.tokens_own), channel_id=1, source_target_pairs={{0,1},{1,0},{2,3},{3,2},{4,5},{5,4},{6,7},{7,6},{8,9},{9,8},{10,11... | collective-permute-start | bytes 2359304 | tf_op jit(solution)/shard_map/ppermute | solution.py:462
  49.0 14.5 %collective-permute-start.10 = (bf16[4,48,1024]{2,1,0:T(8,128)(2,1)S(1)}, bf16[4,48,1024]{2,1,0:T(8,128)(2,1)S(1)}, u32[]{:S(2)}, u32[]{:S(2)}) collective-permute-start(bf16[4,48,1024]{2,1,0:T(8,128)(2,1)S(1)} %order_qkv.1.b0), channel_id=1, source_target_pairs={{0,8},{1,9},{2,10},{3,11},{4,12},{5,13},{6,14},{7,15},{8,0},{9,1},... | collective-permute-start | bytes 1179656 | tf_op jit(solution)/shard_map/ppermute | solution.py:462
  50.2 15.1 %collective-permute-start.11 = (bf16[4,48,1024]{2,1,0:T(8,128)(2,1)S(1)}, bf16[4,48,1024]{2,1,0:T(8,128)(2,1)}, u32[]{:S(2)}, u32[]{:S(2)}) collective-permute-start(bf16[4,48,1024]{2,1,0:T(8,128)(2,1)S(1)} %order_qkv.1.b0), channel_id=1, source_target_pairs={{0,16},{1,17},{2,18},{3,19},{4,20},{5,21},{6,22},{7,23},{8,24},{9,... | collective-permute-start | bytes 1179656 | tf_op jit(solution)/shard_map/ppermute | solution.py:462
  51.5 21.3 %collective-permute-start.12 = (bf16[4,48,1024]{2,1,0:T(8,128)(2,1)S(1)}, bf16[4,48,1024]{2,1,0:T(8,128)(2,1)}, u32[]{:S(2)}, u32[]{:S(2)}) collective-permute-start(bf16[4,48,1024]{2,1,0:T(8,128)(2,1)S(1)} %order_qkv.1.b0), channel_id=1, source_target_pairs={{0,24},{1,25},{2,26},{3,27},{4,28},{5,29},{6,30},{7,31},{8,16},{9,... | collective-permute-start | bytes 1179656 | tf_op jit(solution)/shard_map/ppermute | solution.py:462
  52.2 32.3 %collective-permute-start.16 = (bf16[48,1536]{1,0:T(8,128)(2,1)S(1)}, bf16[48,1536]{1,0:T(8,128)(2,1)S(1)}, u32[]{:S(2)}, u32[]{:S(2)}) collective-permute-start(bf16[48,1536]{1,0:T(8,128)(2,1)S(1)} %pad_maximum_fusion.2.own), channel_id=1, source_target_pairs={{0,2},{1,3},{2,4},{3,5},{4,6},{5,7},{6,0},{7,1},{8,10},{9,11},{10,... | collective-permute-start | bytes 442376 | tf_op jit(solution)/shard_map/ppermute | solution.py:462
  63.5 21.0 %collective-permute-start.17 = (bf16[48,1536]{1,0:T(8,128)(2,1)S(1)}, bf16[48,1536]{1,0:T(8,128)(2,1)S(1)}, u32[]{:S(2)}, u32[]{:S(2)}) collective-permute-start(bf16[48,1536]{1,0:T(8,128)(2,1)S(1)} %pad_maximum_fusion.2.own), channel_id=1, source_target_pairs={{0,4},{1,5},{2,6},{3,7},{4,0},{5,1},{6,2},{7,3},{8,12},{9,13},{10,... | collective-permute-start | bytes 442376 | tf_op jit(solution)/shard_map/ppermute | solution.py:462
  65.3 19.2 %collective-permute-start.18 = (bf16[48,1536]{1,0:T(8,128)(2,1)S(1)}, bf16[48,1536]{1,0:T(8,128)(2,1)S(1)}, u32[]{:S(2)}, u32[]{:S(2)}) collective-permute-start(bf16[48,1536]{1,0:T(8,128)(2,1)S(1)} %pad_maximum_fusion.2.own), channel_id=1, source_target_pairs={{0,6},{1,7},{2,0},{3,1},{4,2},{5,3},{6,4},{7,5},{8,14},{9,15},{10,... | collective-permute-start | bytes 442376 | tf_op jit(solution)/shard_map/ppermute | solution.py:462
  86.2 21.6 %collective-permute-start.22 = (bf16[192,1536]{1,0:T(8,128)(2,1)S(1)}, bf16[192,1536]{1,0:T(8,128)(2,1)}, u32[]{:S(2)}, u32[]{:S(2)}) collective-permute-start(bf16[192,1536]{1,0:T(8,128)(2,1)S(1)} %bitcast.104), channel_id=1, source_target_pairs={{0,8},{1,9},{2,10},{3,11},{4,12},{5,13},{6,14},{7,15},{8,0},{9,1},... | collective-permute-start | bytes 1769480 | tf_op jit(solution)/shard_map/ppermute | solution.py:462
  86.6 21.2 %collective-permute-start.23 = (bf16[192,1536]{1,0:T(8,128)(2,1)S(1)}, bf16[192,1536]{1,0:T(8,128)(2,1)}, u32[]{:S(2)}, u32[]{:S(2)}) collective-permute-start(bf16[192,1536]{1,0:T(8,128)(2,1)S(1)} %bitcast.105), channel_id=1, source_target_pairs={{0,16},{1,17},{2,18},{3,19},{4,20},{5,21},{6,22},{7,23},{8,24},{9,... | collective-permute-start | bytes 1769480 | tf_op jit(solution)/shard_map/ppermute | solution.py:462
  109.5 20.1 %collective-permute-start.24 = (bf16[96,1536]{1,0:T(8,128)(2,1)}, bf16[96,1536]{1,0:T(8,128)(2,1)}, u32[]{:S(2)}, u32[]{:S(2)}) collective-permute-start(bf16[96,1536]{1,0:T(8,128)(2,1)} %slice.114), channel_id=1, source_target_pairs={{0,8},{1,9},{2,10},{3,11},{4,12},{5,13},{6,14},{7,15},{8,0},{9,1},... | collective-permute-start | bytes 884744 | tf_op jit(solution)/shard_map/ppermute | solution.py:462
  111.5 18.0 %collective-permute-start.25 = (bf16[96,1536]{1,0:T(8,128)(2,1)}, bf16[96,1536]{1,0:T(8,128)(2,1)}, u32[]{:S(2)}, u32[]{:S(2)}) collective-permute-start(bf16[96,1536]{1,0:T(8,128)(2,1)} %slice.115), channel_id=1, source_target_pairs={{0,16},{1,17},{2,18},{3,19},{4,20},{5,21},{6,22},{7,23},{8,24},{9,... | collective-permute-start | bytes 884744 | tf_op jit(solution)/shard_map/ppermute | solution.py:462
  142.3 18.3 %collective-permute-start.35 = (bf16[96,1536]{1,0:T(8,128)(2,1)S(1)}, bf16[96,1536]{1,0:T(8,128)(2,1)S(1)}, u32[]{:S(2)}, u32[]{:S(2)}) collective-permute-start(bf16[96,1536]{1,0:T(8,128)(2,1)S(1)} %get-tuple-element.159), channel_id=1, source_target_pairs={{0,8},{1,9},{2,10},{3,11},{4,12},{5,13},{6,14},{7,15},{8,0},{9,1},... | collective-permute-start | bytes 884744 | tf_op jit(solution)/shard_map/ppermute | solution.py:462
  142.6 18.0 %collective-permute-start.36 = (bf16[96,1536]{1,0:T(8,128)(2,1)S(1)}, bf16[96,1536]{1,0:T(8,128)(2,1)S(1)}, u32[]{:S(2)}, u32[]{:S(2)}) collective-permute-start(bf16[96,1536]{1,0:T(8,128)(2,1)S(1)} %get-tuple-element.160), channel_id=1, source_target_pairs={{0,16},{1,17},{2,18},{3,19},{4,20},{5,21},{6,22},{7,23},{8,24},{9,... | collective-permute-start | bytes 884744 | tf_op jit(solution)/shard_map/ppermute | solution.py:462
  162.3 47.4 %collective-permute-start.55 = (bf16[192,1536]{1,0:T(8,128)(2,1)}, bf16[192,1536]{1,0:T(8,128)(2,1)}, u32[]{:S(2)}, u32[]{:S(2)}) collective-permute-start(bf16[192,1536]{1,0:T(8,128)(2,1)} %get-tuple-element.195), channel_id=1, source_target_pairs={{0,8},{1,9},{2,10},{3,11},{4,12},{5,13},{6,14},{7,15},{8,0},{9,1},... | collective-permute-start | bytes 1769480 | tf_op jit(solution)/shard_map/ppermute | solution.py:462
  162.7 47.0 %collective-permute-start.56 = (bf16[192,1536]{1,0:T(8,128)(2,1)}, bf16[192,1536]{1,0:T(8,128)(2,1)}, u32[]{:S(2)}, u32[]{:S(2)}) collective-permute-start(bf16[192,1536]{1,0:T(8,128)(2,1)} %get-tuple-element.227), channel_id=1, source_target_pairs={{0,16},{1,17},{2,18},{3,19},{4,20},{5,21},{6,22},{7,23},{8,24},{9,... | collective-permute-start | bytes 1769480 | tf_op jit(solution)/shard_map/ppermute | solution.py:462
  169.0 38.4 %collective-permute-start.50 = (bf16[96,1920]{1,0:T(8,128)(2,1)}, bf16[96,1920]{1,0:T(8,128)(2,1)}, u32[]{:S(2)}, u32[]{:S(2)}) collective-permute-start(bf16[96,1920]{1,0:T(8,128)(2,1)} %get-tuple-element.191), channel_id=1, source_target_pairs={{0,8},{1,9},{2,10},{3,11},{4,12},{5,13},{6,14},{7,15},{8,0},{9,1},... | collective-permute-start | bytes 1105928 | tf_op jit(solution)/shard_map/ppermute | solution.py:462
  169.3 38.1 %collective-permute-start.51 = (bf16[96,1920]{1,0:T(8,128)(2,1)}, bf16[96,1920]{1,0:T(8,128)(2,1)}, u32[]{:S(2)}, u32[]{:S(2)}) collective-permute-start(bf16[96,1920]{1,0:T(8,128)(2,1)} %get-tuple-element.192), channel_id=1, source_target_pairs={{0,16},{1,17},{2,18},{3,19},{4,20},{5,21},{6,22},{7,23},{8,24},{9,... | collective-permute-start | bytes 1105928 | tf_op jit(solution)/shard_map/ppermute | solution.py:462
  212.5 80.6 %reduce-scatter.3.cloned.1.call-start = ((), (), s32[]{:S(2)}) async-start(), calls=%async_computation.3 | async-start | bytes 921600 | tf_op jit(solution)/shard_map/reduce_scatter | solution.py:492
  214.1 31.9 %collective-permute-start.52 = (bf16[192,1920]{1,0:T(8,128)(2,1)}, bf16[192,1920]{1,0:T(8,128)(2,1)S(1)}, u32[]{:S(2)}, u32[]{:S(2)}) collective-permute-start(bf16[192,1920]{1,0:T(8,128)(2,1)} %copy-done.63), channel_id=1, source_target_pairs={{0,8},{1,9},{2,10},{3,11},{4,12},{5,13},{6,14},{7,15},{8,0},{9,1},... | collective-permute-start | bytes 2211848 | tf_op jit(solution)/shard_map/ppermute | solution.py:462
  214.5 31.6 %collective-permute-start.53 = (bf16[192,1920]{1,0:T(8,128)(2,1)}, bf16[192,1920]{1,0:T(8,128)(2,1)S(1)}, u32[]{:S(2)}, u32[]{:S(2)}) collective-permute-start(bf16[192,1920]{1,0:T(8,128)(2,1)} %copy-done.62), channel_id=1, source_target_pairs={{0,16},{1,17},{2,18},{3,19},{4,20},{5,21},{6,22},{7,23},{8,24},{9,... | collective-permute-start | bytes 2211848 | tf_op jit(solution)/shard_map/ppermute | solution.py:462
  218.1 19.1 %collective-permute-start.43 = (bf16[192,640]{1,0:T(8,128)(2,1)S(1)}, bf16[192,640]{1,0:T(8,128)(2,1)S(1)}, u32[]{:S(2)}, u32[]{:S(2)}) collective-permute-start(bf16[192,640]{1,0:T(8,128)(2,1)S(1)} %copy-done.71), channel_id=1, source_target_pairs={{0,8},{1,9},{2,10},{3,11},{4,12},{5,13},{6,14},{7,15},{8,0},{9,1},... | collective-permute-start | bytes 737288 | tf_op jit(solution)/shard_map/ppermute | solution.py:462
  218.4 18.9 %collective-permute-start.44 = (bf16[192,640]{1,0:T(8,128)(2,1)S(1)}, bf16[192,640]{1,0:T(8,128)(2,1)S(1)}, u32[]{:S(2)}, u32[]{:S(2)}) collective-permute-start(bf16[192,640]{1,0:T(8,128)(2,1)S(1)} %copy-done.69), channel_id=1, source_target_pairs={{0,16},{1,17},{2,18},{3,19},{4,20},{5,21},{6,22},{7,23},{8,24},{9,... | collective-permute-start | bytes 737288 | tf_op jit(solution)/shard_map/ppermute | solution.py:462
  219.3 23.5 %collective-permute-start.45 = (bf16[192,640]{1,0:T(8,128)(2,1)S(1)}, bf16[192,640]{1,0:T(8,128)(2,1)S(1)}, u32[]{:S(2)}, u32[]{:S(2)}) collective-permute-start(bf16[192,640]{1,0:T(8,128)(2,1)S(1)} %copy-done.67), channel_id=1, source_target_pairs={{0,24},{1,25},{2,26},{3,27},{4,28},{5,29},{6,30},{7,31},{8,16},{9,... | collective-permute-start | bytes 737288 | tf_op jit(solution)/shard_map/ppermute | solution.py:462
  253.8 12.6 %collective-permute-start.48 = (bf16[48,640]{1,0:T(8,128)(2,1)S(1)}, bf16[48,640]{1,0:T(8,128)(2,1)S(1)}, u32[]{:S(2)}, u32[]{:S(2)}) collective-permute-start(bf16[48,640]{1,0:T(8,128)(2,1)S(1)} %copy-done.74), channel_id=1, source_target_pairs={{0,6},{1,7},{2,0},{3,1},{4,2},{5,3},{6,4},{7,5},{8,14},{9,15},{10,... | collective-permute-start | bytes 184328 | tf_op jit(solution)/shard_map/ppermute | solution.py:462
  256.0 33.1 %collective-permute-start.40 = (bf16[128,768]{1,0:T(8,128)(2,1)}, bf16[128,768]{1,0:T(8,128)(2,1)S(1)}, u32[]{:S(2)}, u32[]{:S(2)}) collective-permute-start(bf16[128,768]{1,0:T(8,128)(2,1)} %get-tuple-element.245), channel_id=1, source_target_pairs={{0,2},{1,3},{2,4},{3,5},{4,6},{5,7},{6,0},{7,1},{8,10},{9,11},{10,... | collective-permute-start | bytes 589832 | tf_op jit(solution)/shard_map/ppermute | solution.py:462
  256.1 33.0 %collective-permute-start.41 = (bf16[128,768]{1,0:T(8,128)(2,1)}, bf16[128,768]{1,0:T(8,128)(2,1)S(1)}, u32[]{:S(2)}, u32[]{:S(2)}) collective-permute-start(bf16[128,768]{1,0:T(8,128)(2,1)} %get-tuple-element.244), channel_id=1, source_target_pairs={{0,4},{1,5},{2,6},{3,7},{4,0},{5,1},{6,2},{7,3},{8,12},{9,13},{10,... | collective-permute-start | bytes 589832 | tf_op jit(solution)/shard_map/ppermute | solution.py:462
  258.1 31.0 %collective-permute-start.42 = (bf16[128,768]{1,0:T(8,128)(2,1)}, bf16[128,768]{1,0:T(8,128)(2,1)}, u32[]{:S(2)}, u32[]{:S(2)}) collective-permute-start(bf16[128,768]{1,0:T(8,128)(2,1)} %get-tuple-element.243), channel_id=1, source_target_pairs={{0,6},{1,7},{2,0},{3,1},{4,2},{5,3},{6,4},{7,5},{8,14},{9,15},{10,... | collective-permute-start | bytes 589832 | tf_op jit(solution)/shard_map/ppermute | solution.py:462
  267.8 11.6 %collective-permute-start.49 = (f32[24,1280]{1,0:T(8,128)}, f32[24,1280]{1,0:T(8,128)}, u32[]{:S(2)}, u32[]{:S(2)}) collective-permute-start(f32[24,1280]{1,0:T(8,128)} %constant_dynamic-slice_fusion.2), channel_id=1, source_target_pairs={{0,1},{1,0},{2,3},{3,2},{4,5},{5,4},{6,7},{7,6},{8,9},{9,8},{10,11... | collective-permute-start | bytes 368648 | tf_op jit(solution)/shard_map/ppermute | solution.py:462
  (120 other events, 668.7 us)
Sparse Core Ops, SparseCore 0:
  14.3 74.4 all-gather.1
  212.6 20.4 reduce-scatter.4
  247.9 38.9 reduce-scatter.2
